TPU v7x, 32 devices: a whole 2x2x4 slice. The times are simulated.
32 devices in a mesh: rows: 8 (over z, x), feat: 4 (over y, core).
Axes of the slice: x: 2, y: 2, z: 4, core: 2. Of those that a mesh axis runs over, the one named last changes fastest.
Arguments:
- features: float32 [8192, 512], P('rows', 'feat')
- counts: int32 [8], P('rows'), may hold values from 256 to 1024, as said below
- validity: int32 [8192], P('rows'), may hold values from 0 to 1, as said below
- mask_logits: float32 [6, 512], P(None, 'feat'), may hold values from -4 to 4
- w_update: float32 [6, 1024, 512], P(None, None, 'feat'), may hold values from -0.1875 to 0.1875
- w_reset: float32 [6, 1024, 512], P(None, None, 'feat'), may hold values from -0.1875 to 0.1875
- w_candidate: float32 [6, 1024, 512], P(None, None, 'feat'), may hold values from -0.1875 to 0.1875
- b_update: float32 [6, 512], P(None, 'feat'), may hold values from -3 to 3
- b_reset: float32 [6, 512], P(None, 'feat'), may hold values from -3 to 3
- b_candidate: float32 [6, 512], P(None, 'feat'), may hold values from -3 to 3
- norm_gain: float32 [512], P('feat'), may hold values from 0.5 to 1.5
- norm_shift: float32 [512], P('feat'), may hold values from -3 to 3
- w_head: float32 [512, 256], P('feat'), may hold values from -0.25 to 0.25
- b_head: float32 [256], replicated, may hold values from -3 to 3
- w_out: float32 [256, 10], replicated, may hold values from -0.75 to 0.75
- b_out: float32 [10], replicated, may hold values from -3 to 3
- cotangent: float32 [8192, 10], P('rows'), may hold values from -6 to 6
Outputs:
- logits: float32 [8192, 10], P('rows')
- grad_features: float32 [8192, 512], P('rows', 'feat')
- grad_mask: float32 [6, 512], P(None, 'feat')
- grad_w_update: float32 [6, 1024, 512], P(None, None, 'feat')
- grad_w_reset: float32 [6, 1024, 512], P(None, None, 'feat')
- grad_w_candidate: float32 [6, 1024, 512], P(None, None, 'feat')
- grad_b_update: float32 [6, 512], P(None, 'feat')
- grad_b_reset: float32 [6, 512], P(None, 'feat')
- grad_b_candidate: float32 [6, 512], P(None, 'feat')
- grad_norm_gain: float32 [512], P('feat')
- grad_norm_shift: float32 [512], P('feat')
- grad_w_head: float32 [512, 256], P('feat')
- grad_b_head: float32 [256], replicated
- grad_w_out: float32 [256, 10], replicated
- grad_b_out: float32 [10], replicated
Inputs may be any that keep to these rules, and one draw needn't show every extreme that they name: Device d of the rows axis has counts[d] filled rows at the start of its block of 1024 rows, the rest being padding; in every draw some device is full. `validity`: the first row of each device's block of 1024 rows is 1.
All inputs are finite; a program needn't handle non-finite values.
Results may differ from a plain program's by a relative error of at most 0.0003.
Values sent between devices are 32-bit elements; how exact they have to be, the bound alone decides.
A program may use at most 192 MiB of HBM per device.

v0:
```python
import jax
import jax.numpy as jnp
from jax import lax
from jax.sharding import PartitionSpec as P


def matmul(left_side, right_side):
    return jnp.dot(
        left_side, right_side, precision=lax.Precision.HIGHEST, preferred_element_type=jnp.float32
    )


def mul_trans(left_side, right_side):
    return lax.dot_general(
        left_side,
        right_side,
        (((1,), (1,)), ((), ())),
        precision=lax.Precision.HIGHEST,
        preferred_element_type=jnp.float32,
    )


def trans_mul(left_side, right_side):
    return lax.dot_general(
        left_side,
        right_side,
        (((0,), (0,)), ((), ())),
        precision=lax.Precision.HIGHEST,
        preferred_element_type=jnp.float32,
    )


def exact_gelu(argument):
    return jax.nn.gelu(argument, approximate=False)


def local(
    features,
    counts,
    validity,
    mask_logits,
    w_update,
    w_reset,
    w_candidate,
    b_update,
    b_reset,
    b_candidate,
    norm_gain,
    norm_shift,
    w_head,
    b_head,
    w_out,
    b_out,
    cotangent,
):
    row_slots, block_cols = features.shape
    sections = w_update.shape[0]
    filled = (jnp.arange(row_slots) < counts[0]).astype(jnp.float32)
    column = (filled * validity.astype(jnp.float32))[:, None]
    x_all, logit_all = (
        lax.all_gather(features, "feat", axis=1, tiled=True),
        lax.all_gather(mask_logits, "feat", axis=1, tiled=True),
    )
    width = x_all.shape[1]
    mask_probs = jax.nn.softmax(logit_all, axis=1)
    mask_scale = width * mask_probs
    offset = lax.axis_index("feat") * block_cols
    probs_own = lax.dynamic_slice_in_dim(mask_probs, offset, block_cols, 1)
    scale_own = width * probs_own
    current = features
    saved = []
    for section_num in range(sections):
        h_all = lax.all_gather(current, "feat", axis=1, tiled=True)
        scaled = x_all * mask_scale[section_num]
        upper = jnp.concatenate([h_all, scaled], 1)
        update = jax.nn.sigmoid(matmul(upper, w_update[section_num]) + b_update[section_num])
        resets = jax.nn.sigmoid(matmul(upper, w_reset[section_num]) + b_reset[section_num])
        r_all = lax.all_gather(resets * current, "feat", axis=1, tiled=True)
        lower = jnp.concatenate([r_all, scaled], 1)
        candidate = jnp.tanh(matmul(lower, w_candidate[section_num]) + b_candidate[section_num])
        saved.append((current,))
        current = current + update * (candidate - current)
    col_sums, count_all = lax.psum((jnp.sum(column * current, 0), jnp.sum(column)), "rows")
    col_mean = col_sums / count_all
    centered = current - col_mean
    spread = lax.psum(jnp.sum(column * centered * centered, 0), "rows")
    inv_std = lax.rsqrt(spread / count_all + 1e-05)
    x_hat = centered * inv_std
    normed = x_hat * norm_gain + norm_shift
    pre_act = lax.psum(matmul(normed, w_head), "feat") + b_head
    hidden, gelu_back = jax.vjp(exact_gelu, pre_act)
    logits = (matmul(hidden, w_out) + b_out) * column
    d_logits = cotangent * column
    g_w_out = trans_mul(hidden, d_logits)
    g_b_out = jnp.sum(d_logits, 0)
    d_act = gelu_back(mul_trans(d_logits, w_out))[0]
    g_w_head = trans_mul(normed, d_act)
    g_b_head = jnp.sum(d_act, 0)
    d_normed = mul_trans(d_act, w_head)
    grad_norm_gain, grad_norm_shift = lax.psum(
        (jnp.sum(d_normed * x_hat, 0), jnp.sum(d_normed, 0)), "rows"
    )
    d_state = inv_std * (
        d_normed * norm_gain
        - column / count_all * norm_gain * (grad_norm_shift + x_hat * grad_norm_gain)
    )
    grad_input = jnp.zeros_like(features)
    list_wz = [None] * sections
    list_wr = [None] * sections
    list_wo = [None] * sections
    list_bz = [None] * sections
    list_br = [None] * sections
    list_bo = [None] * sections
    list_gsc = [None] * sections
    for section_num in reversed(range(sections)):
        previous = saved[section_num][0]
        h_all = lax.all_gather(previous, "feat", axis=1, tiled=True)
        scaled = x_all * mask_scale[section_num]
        upper = jnp.concatenate([h_all, scaled], 1)
        update = jax.nn.sigmoid(matmul(upper, w_update[section_num]) + b_update[section_num])
        resets = jax.nn.sigmoid(matmul(upper, w_reset[section_num]) + b_reset[section_num])
        r_all = lax.all_gather(resets * previous, "feat", axis=1, tiled=True)
        lower = jnp.concatenate([r_all, scaled], 1)
        candidate = jnp.tanh(matmul(lower, w_candidate[section_num]) + b_candidate[section_num])
        d_cand = d_state * update * (1.0 - candidate * candidate)
        d_update = d_state * (candidate - previous) * update * (1.0 - update)
        dlower = mul_trans(d_cand, w_candidate[section_num])
        dreset_h, dxs_out = (
            lax.psum_scatter(dlower[:, :width], "feat", scatter_dimension=1, tiled=True),
            lax.psum_scatter(dlower[:, width:], "feat", scatter_dimension=1, tiled=True),
        )
        d_resets = dreset_h * previous * resets * (1.0 - resets)
        dupper = mul_trans(d_update, w_update[section_num]) + mul_trans(
            d_resets, w_reset[section_num]
        )
        dh_up, dxs_in = (
            lax.psum_scatter(dupper[:, :width], "feat", scatter_dimension=1, tiled=True),
            lax.psum_scatter(dupper[:, width:], "feat", scatter_dimension=1, tiled=True),
        )
        d_scaled = dxs_in + dxs_out
        list_gsc[section_num] = jnp.sum(d_scaled * features, 0)
        grad_input = grad_input + d_scaled * scale_own[section_num]
        list_wz[section_num] = trans_mul(upper, d_update)
        list_wr[section_num] = trans_mul(upper, d_resets)
        list_wo[section_num] = trans_mul(lower, d_cand)
        list_bz[section_num] = jnp.sum(d_update, 0)
        list_br[section_num] = jnp.sum(d_resets, 0)
        list_bo[section_num] = jnp.sum(d_cand, 0)
        d_state = d_state * (1.0 - update) + dreset_h * resets + dh_up
    grad_input = grad_input + d_state
    gsc_stack = jnp.stack(list_gsc)
    summed = lax.psum(
        (
            jnp.stack(list_wz),
            jnp.stack(list_wr),
            jnp.stack(list_wo),
            jnp.stack(list_bz),
            jnp.stack(list_br),
            jnp.stack(list_bo),
            gsc_stack,
            g_w_head,
            g_b_head,
            g_w_out,
            g_b_out,
        ),
        "rows",
    )
    (
        grad_wz_all,
        grad_wr_all,
        grad_wo_all,
        grad_bz_all,
        grad_br_all,
        grad_bo_all,
        gsc_total,
        grad_head_w,
        grad_head_b,
        grad_out_w,
        grad_out_b,
    ) = summed
    inner_sum = lax.psum(jnp.sum(probs_own * gsc_total, 1), "feat")
    grad_mask = width * probs_own * (gsc_total - inner_sum[:, None])
    return (
        logits,
        grad_input,
        grad_mask,
        grad_wz_all,
        grad_wr_all,
        grad_wo_all,
        grad_bz_all,
        grad_br_all,
        grad_bo_all,
        grad_norm_gain,
        grad_norm_shift,
        grad_head_w,
        grad_head_b,
        grad_out_w,
        grad_out_b,
    )


def solution(mesh):
    return jax.shard_map(
        local,
        mesh=mesh,
        in_specs=(
            P("rows", "feat"),
            P("rows"),
            P("rows"),
            P(None, "feat"),
            P(None, None, "feat"),
            P(None, None, "feat"),
            P(None, None, "feat"),
            P(None, "feat"),
            P(None, "feat"),
            P(None, "feat"),
            P("feat"),
            P("feat"),
            P("feat", None),
            P(),
            P(),
            P(),
            P("rows", None),
        ),
        out_specs=(
            P("rows", None),
            P("rows", "feat"),
            P(None, "feat"),
            P(None, None, "feat"),
            P(None, None, "feat"),
            P(None, None, "feat"),
            P(None, "feat"),
            P(None, "feat"),
            P(None, "feat"),
            P("feat"),
            P("feat"),
            P("feat", None),
            P(),
            P(),
            P(),
        ),
        check_vma=False,
    )
```

profile of v0, /device:TPU:0, one launch (start us, length us, event | category | flops | bytes accessed | tf_op | source)
XLA Modules:
  0.0 1545.9 jit_solution(1256925565031716170)
XLA Ops:
  47.4 22.9 %all-gather.15.cloned.1.call-done = f32[1024,512]{1,0:T(8,128)} async-done(((f32[1024,128]{1,0:T(8,128)}), f32[1024,512]{1,0:T(8,128)}) %all-gather.15.cloned.1.call-update) | async-done | bytes 2097168 | tf_op jit(solution)/shard_map/all_gather | solution.py:78
  81.7 22.7 %all-gather.17.cloned.1.call-done = f32[1024,512]{1,0:T(8,128)} async-done(((f32[1024,128]{1,0:T(8,128)}), f32[1024,512]{1,0:T(8,128)}) %all-gather.17.cloned.1.call-update) | async-done | bytes 2097168 | tf_op jit(solution)/shard_map/all_gather | solution.py:73
  111.4 22.9 %all-gather.19.cloned.1.call-done = f32[1024,512]{1,0:T(8,128)} async-done(((f32[1024,128]{1,0:T(8,128)}), f32[1024,512]{1,0:T(8,128)}) %all-gather.19.cloned.1.call-update) | async-done | bytes 2097168 | tf_op jit(solution)/shard_map/all_gather | solution.py:78
  146.1 22.5 %all-gather.21.cloned.1.call-done = f32[1024,512]{1,0:T(8,128)} async-done(((f32[1024,128]{1,0:T(8,128)}), f32[1024,512]{1,0:T(8,128)}) %all-gather.21.cloned.1.call-update) | async-done | bytes 2097168 | tf_op jit(solution)/shard_map/all_gather | solution.py:73
  175.6 22.9 %all-gather.23.cloned.1.call-done = f32[1024,512]{1,0:T(8,128)} async-done(((f32[1024,128]{1,0:T(8,128)}), f32[1024,512]{1,0:T(8,128)}) %all-gather.23.cloned.1.call-update) | async-done | bytes 2097168 | tf_op jit(solution)/shard_map/all_gather | solution.py:78
  210.1 22.8 %all-gather.25.cloned.1.call-done = f32[1024,512]{1,0:T(8,128)} async-done(((f32[1024,128]{1,0:T(8,128)}), f32[1024,512]{1,0:T(8,128)}) %all-gather.25.cloned.1.call-update) | async-done | bytes 2097168 | tf_op jit(solution)/shard_map/all_gather | solution.py:73
  239.8 22.9 %all-gather.27.cloned.1.call-done = f32[1024,512]{1,0:T(8,128)} async-done(((f32[1024,128]{1,0:T(8,128)}), f32[1024,512]{1,0:T(8,128)}) %all-gather.27.cloned.1.call-update) | async-done | bytes 2097168 | tf_op jit(solution)/shard_map/all_gather | solution.py:78
  274.3 22.7 %all-gather.29.cloned.1.call-done = f32[1024,512]{1,0:T(8,128)} async-done(((f32[1024,128]{1,0:T(8,128)}), f32[1024,512]{1,0:T(8,128)}) %all-gather.29.cloned.1.call-update) | async-done | bytes 2097168 | tf_op jit(solution)/shard_map/all_gather | solution.py:73
  304.0 22.9 %all-gather.31.cloned.1.call-done = f32[1024,512]{1,0:T(8,128)} async-done(((f32[1024,128]{1,0:T(8,128)}), f32[1024,512]{1,0:T(8,128)}) %all-gather.31.cloned.1.call-update) | async-done | bytes 2097168 | tf_op jit(solution)/shard_map/all_gather | solution.py:78
  338.7 22.5 %all-gather.33.cloned.1.call-done = f32[1024,512]{1,0:T(8,128)} async-done(((f32[1024,128]{1,0:T(8,128)}), f32[1024,512]{1,0:T(8,128)}) %all-gather.33.cloned.1.call-update) | async-done | bytes 2097168 | tf_op jit(solution)/shard_map/all_gather | solution.py:73
  401.7 22.0 %all-reduce.2 = (f32[128]{0:T(128)S(1)}, f32[]{:T(128)}) all-reduce(f32[128]{0:T(128)S(1)} %get-tuple-element.83, f32[]{:T(128)} %get-tuple-element.81), channel_id=1, replica_groups=mesh['rows'=8,'feat'=4] {'rows'}, use_global_device_ids=true, to_apply=%region_3.0 | all-reduce | flops 129 | bytes 1032 | tf_op jit(solution)/shard_map/psum | solution.py:83
  445.3 33.3 %all-reduce.7.cloned.1.call-done = f32[1024,256]{1,0:T(8,128)} async-done(((f32[1024,256]{1,0:T(8,128)}), f32[1024,256]{1,0:T(8,128)}) %all-reduce.7.cloned.1.call-update) | async-done | bytes 1048592 | tf_op jit(solution)/shard_map/psum | solution.py:90
  558.8 31.6 %reduce-scatter.21.cloned.1.call-done = f32[1024,128]{1,0:T(8,128)} async-done(((f32[1024,512]{1,0:T(8,128)}), f32[1024,128]{1,0:T(8,128)}) %reduce-scatter.21.cloned.1.call-update) | async-done | bytes 524304 | tf_op jit(solution)/shard_map/reduce_scatter | solution.py:137
  602.9 31.1 %reduce-scatter.23.cloned.1.call-done = f32[1024,128]{1,0:T(8,128)} async-done(((f32[1024,512]{1,0:T(8,128)}), f32[1024,128]{1,0:T(8,128)}) %reduce-scatter.23.cloned.1.call-update) | async-done | bytes 524304 | tf_op jit(solution)/shard_map/reduce_scatter | solution.py:129
  648.9 31.4 %reduce-scatter.25.cloned.1.call-done = f32[1024,128]{1,0:T(8,128)} async-done(((f32[1024,512]{1,0:T(8,128)}), f32[1024,128]{1,0:T(8,128)}) %reduce-scatter.25.cloned.1.call-update) | async-done | bytes 524304 | tf_op jit(solution)/shard_map/reduce_scatter | solution.py:137
  700.6 23.1 %reduce-scatter.27.cloned.1.call-done = f32[1024,128]{1,0:T(8,128)} async-done(((f32[1024,512]{1,0:T(8,128)}), f32[1024,128]{1,0:T(8,128)}) %reduce-scatter.27.cloned.1.call-update) | async-done | bytes 524304 | tf_op jit(solution)/shard_map/reduce_scatter | solution.py:129
  734.8 31.3 %reduce-scatter.29.cloned.1.call-done = f32[1024,128]{1,0:T(8,128)} async-done(((f32[1024,512]{1,0:T(8,128)}), f32[1024,128]{1,0:T(8,128)}) %reduce-scatter.29.cloned.1.call-update) | async-done | bytes 524304 | tf_op jit(solution)/shard_map/reduce_scatter | solution.py:137
  786.4 23.2 %reduce-scatter.31.cloned.1.call-done = f32[1024,128]{1,0:T(8,128)} async-done(((f32[1024,512]{1,0:T(8,128)}), f32[1024,128]{1,0:T(8,128)}) %reduce-scatter.31.cloned.1.call-update) | async-done | bytes 524304 | tf_op jit(solution)/shard_map/reduce_scatter | solution.py:129
  820.5 31.3 %reduce-scatter.33.cloned.1.call-done = f32[1024,128]{1,0:T(8,128)} async-done(((f32[1024,512]{1,0:T(8,128)}), f32[1024,128]{1,0:T(8,128)}) %reduce-scatter.33.cloned.1.call-update) | async-done | bytes 524304 | tf_op jit(solution)/shard_map/reduce_scatter | solution.py:137
  872.1 23.2 %reduce-scatter.35.cloned.1.call-done = f32[1024,128]{1,0:T(8,128)} async-done(((f32[1024,512]{1,0:T(8,128)}), f32[1024,128]{1,0:T(8,128)}) %reduce-scatter.35.cloned.1.call-update) | async-done | bytes 524304 | tf_op jit(solution)/shard_map/reduce_scatter | solution.py:129
  906.4 31.1 %reduce-scatter.37.cloned.1.call-done = f32[1024,128]{1,0:T(8,128)} async-done(((f32[1024,512]{1,0:T(8,128)}), f32[1024,128]{1,0:T(8,128)}) %reduce-scatter.37.cloned.1.call-update) | async-done | bytes 524304 | tf_op jit(solution)/shard_map/reduce_scatter | solution.py:137
  1150.9 34.0 %reduce-scatter.53.cloned.1.call-done = f32[1024,128]{1,0:T(8,128)} async-done(((f32[1024,512]{1,0:T(8,128)}), f32[1024,128]{1,0:T(8,128)}) %reduce-scatter.53.cloned.1.call-update) | async-done | bytes 524304 | tf_op jit(solution)/shard_map/reduce_scatter | solution.py:138
  1187.0 38.0 %all-reduce = (f32[6,128]{1,0:T(8,128)S(1)}, f32[6,128]{1,0:T(8,128)}, f32[6,128]{1,0:T(8,128)}, f32[6,128]{1,0:T(8,128)}, f32[256]{0:T(256)}, /*index=5*/f32[256,10]{0,1:T(8,128)}, f32[10]{0:T(128)}) all-reduce(f32[6,128]{1,0:T(8,128)S(1)} %stack.153, f32[6,128]{1,0:T(8,128)S(1)} %stack.181, ...), channel_id=1, replica_groups=mesh['rows'=8,'feat'=4] {'rows'}, use_global_device_ids=true, to_apply=%region_43.0 | all-reduce | flops 5898 | bytes 47184 | tf_op jit(solution)/shard_map/psum | solution.py:152
  1237.0 292.9 %all-reduce.9.cloned.1.call-done = (f32[6,1024,128]{2,1,0:T(8,128)}, f32[6,1024,128]{2,1,0:T(8,128)}, f32[6,1024,128]{2,1,0:T(8,128)}, f32[128,256]{1,0:T(8,128)}) async-done(((f32[6,1024,128]{2,1,0:T(8,128)}, f32[6,1024,128]{2,1,0:T(8,128)}, f32[6,1024,128]{2,1,0:T(8,128)}, f32[128,256]{1,0:T(8,128)}), (f32[6,1024,128]{2,1,0:T(8,128)}, f32[6,1024,128]{2,1,0:T(8,128)}, f32[6,1024,128]{2,1,0:T(8,128)}, ...) | async-done | bytes 9568272 | tf_op jit(solution)/shard_map/psum | solution.py:152
  (410 shorter events, 624.2 us)
Async XLA Ops:
  7.9 62.4 %all-gather.15.cloned.1.call-start = ((), (), s32[]{:S(2)}) async-start(), calls=%async_computation.19 | async-start | bytes 2621440 | tf_op jit(solution)/shard_map/all_gather | solution.py:78
  111.3 57.3 %all-gather.21.cloned.1.call-start = ((), (), s32[]{:S(2)}) async-start(), calls=%async_computation.22 | async-start | bytes 2621440 | tf_op jit(solution)/shard_map/all_gather | solution.py:73
  175.5 57.3 %all-gather.25.cloned.1.call-start = ((), (), s32[]{:S(2)}) async-start(), calls=%async_computation.24 | async-start | bytes 2621440 | tf_op jit(solution)/shard_map/all_gather | solution.py:73
  239.7 57.3 %all-gather.29.cloned.1.call-start = ((), (), s32[]{:S(2)}) async-start(), calls=%async_computation.26 | async-start | bytes 2621440 | tf_op jit(solution)/shard_map/all_gather | solution.py:73
  367.5 111.0 %all-reduce.7.cloned.1.call-start = ((), (), s32[]{:S(2)}) async-start(), calls=%async_computation.30 | async-start | bytes 2097152 | tf_op jit(solution)/shard_map/psum | solution.py:90
  444.5 103.5 %reduce-scatter.19.cloned.1.call-start = ((), (), s32[]{:S(2)}) async-start(), calls=%async_computation.31 | async-start | bytes 2621440 | tf_op jit(solution)/shard_map/reduce_scatter | solution.py:129
  519.8 70.5 %reduce-scatter.21.cloned.1.call-start = ((), (), s32[]{:S(2)}) async-start(), calls=%async_computation.32 | async-start | bytes 2621440 | tf_op jit(solution)/shard_map/reduce_scatter | solution.py:137
  558.7 75.3 %reduce-scatter.23.cloned.1.call-start = ((), (), s32[]{:S(2)}) async-start(), calls=%async_computation.33 | async-start | bytes 2621440 | tf_op jit(solution)/shard_map/reduce_scatter | solution.py:129
  602.4 77.9 %reduce-scatter.25.cloned.1.call-start = ((), (), s32[]{:S(2)}) async-start(), calls=%async_computation.34 | async-start | bytes 2621440 | tf_op jit(solution)/shard_map/reduce_scatter | solution.py:137
  648.7 75.1 %reduce-scatter.27.cloned.1.call-start = ((), (), s32[]{:S(2)}) async-start(), calls=%async_computation.35 | async-start | bytes 2621440 | tf_op jit(solution)/shard_map/reduce_scatter | solution.py:129
  692.2 73.9 %reduce-scatter.29.cloned.1.call-start = ((), (), s32[]{:S(2)}) async-start(), calls=%async_computation.36 | async-start | bytes 2621440 | tf_op jit(solution)/shard_map/reduce_scatter | solution.py:137
  734.5 75.1 %reduce-scatter.31.cloned.1.call-start = ((), (), s32[]{:S(2)}) async-start(), calls=%async_computation.37 | async-start | bytes 2621440 | tf_op jit(solution)/shard_map/reduce_scatter | solution.py:129
  778.1 73.8 %reduce-scatter.33.cloned.1.call-start = ((), (), s32[]{:S(2)}) async-start(), calls=%async_computation.38 | async-start | bytes 2621440 | tf_op jit(solution)/shard_map/reduce_scatter | solution.py:137
  820.2 75.1 %reduce-scatter.35.cloned.1.call-start = ((), (), s32[]{:S(2)}) async-start(), calls=%async_computation.39 | async-start | bytes 2621440 | tf_op jit(solution)/shard_map/reduce_scatter | solution.py:129
  863.7 73.8 %reduce-scatter.37.cloned.1.call-start = ((), (), s32[]{:S(2)}) async-start(), calls=%async_computation.40 | async-start | bytes 2621440 | tf_op jit(solution)/shard_map/reduce_scatter | solution.py:137
  905.9 74.9 %reduce-scatter.39.cloned.1.call-start = ((), (), s32[]{:S(2)}) async-start(), calls=%async_computation.41 | async-start | bytes 2621440 | tf_op jit(solution)/shard_map/reduce_scatter | solution.py:129
  949.3 187.4 %reduce-scatter.43.cloned.1.call-start = ((), (), s32[]{:S(2)}) async-start(), calls=%async_computation.43 | async-start | bytes 2621440 | tf_op jit(solution)/shard_map/reduce_scatter | solution.py:138
  950.0 186.6 %reduce-scatter.45.cloned.1.call-start = ((), (), s32[]{:S(2)}) async-start(), calls=%async_computation.44 | async-start | bytes 2621440 | tf_op jit(solution)/shard_map/reduce_scatter | solution.py:138
  950.6 186.1 %reduce-scatter.47.cloned.1.call-start = ((), (), s32[]{:S(2)}) async-start(), calls=%async_computation.45 | async-start | bytes 2621440 | tf_op jit(solution)/shard_map/reduce_scatter | solution.py:138
  951.2 185.5 %reduce-scatter.49.cloned.1.call-start = ((), (), s32[]{:S(2)}) async-start(), calls=%async_computation.46 | async-start | bytes 2621440 | tf_op jit(solution)/shard_map/reduce_scatter | solution.py:138
  951.9 198.9 %reduce-scatter.51.cloned.1.call-start = ((), (), s32[]{:S(2)}) async-start(), calls=%async_computation.47 | async-start | bytes 2621440 | tf_op jit(solution)/shard_map/reduce_scatter | solution.py:138
  952.7 232.2 %reduce-scatter.53.cloned.1.call-start = ((), (), s32[]{:S(2)}) async-start(), calls=%async_computation.48 | async-start | bytes 2621440 | tf_op jit(solution)/shard_map/reduce_scatter | solution.py:138
  991.5 241.9 %reduce-scatter.41.cloned.1.call-start = ((), (), s32[]{:S(2)}) async-start(), calls=%async_computation.42 | async-start | bytes 2621440 | tf_op jit(solution)/shard_map/reduce_scatter | solution.py:137
  1004.5 525.3 %all-reduce.9.cloned.1.call-start = ((), (), s32[]{:S(2)}) async-start(), calls=%async_computation.49 | async-start | bytes 19136512 | tf_op jit(solution)/shard_map/psum | solution.py:152
  (116 other events, 2164.6 us)
Sparse Core Ops, SparseCore 0:
  9.6 25.5 all-gather.12
  47.4 22.8 all-gather.14
  81.5 22.8 all-gather.16
  175.6 22.8 all-gather.22
  444.7 33.8 all-reduce.6
  519.9 28.1 reduce-scatter.18
  558.8 31.4 reduce-scatter.20
  602.5 31.4 reduce-scatter.22
  648.8 31.4 reduce-scatter.24
  692.3 31.4 reduce-scatter.26
  734.6 31.4 reduce-scatter.28
  778.2 31.3 reduce-scatter.30
  820.4 31.4 reduce-scatter.32
  863.8 31.4 reduce-scatter.34
  906.0 31.4 reduce-scatter.36
  949.4 31.4 reduce-scatter.38
  983.4 31.4 reduce-scatter.42
  1017.4 31.4 reduce-scatter.44
  1051.2 31.4 reduce-scatter.46
  1085.4 31.4 reduce-scatter.48
  1119.4 31.4 reduce-scatter.50
  1153.4 31.4 reduce-scatter.52
  1187.4 31.4 reduce-scatter.40
  1225.1 304.6 all-reduce.8
  (8 shorter events, 182.2 us)
where the time goes:
time: 1560 us; the launch traced here: 1550 us
  waiting for transfers between devices  946 us (61%)
  matrix products  353 us (23%)
  blocking collectives  111 us (7%)
  other arithmetic  69.4 us (4%)
  local copies, waits for them, and re-layouts  45.1 us (3%)
  between operations  16.2 us (1%)
    psum x1, waiting for transfers between devices, local(): lax.psum((jnp.stack(list_wz), jnp.stack(list_wr), jnp.stack(list_wo), jnp...  293 us
    reduce_scatter x6, waiting for transfers between devices, local(): lax.psum_scatter(dupper[:, :width], 'feat', scatter_dimension=1, tiled=True)  157 us
    dot_general x20, matrix products, trans_mul(): lax.dot_general(left_side, right_side, (((0,), (0,)), ((), ())), precisio...  142 us
    reduce_scatter x6, waiting for transfers between devices, local(): lax.psum_scatter(dlower[:, :width], 'feat', scatter_dimension=1, tiled=True)  142 us
    all_gather x6, waiting for transfers between devices, local(): r_all = lax.all_gather(resets * current, 'feat', axis=1, tiled=True)  136 us
    all_gather x6, waiting for transfers between devices, local(): h_all = lax.all_gather(current, 'feat', axis=1, tiled=True)  132 us
    dot_general x20, matrix products, matmul(): jnp.dot(left_side, right_side, precision=lax.Precision.HIGHEST, preferred...  110 us
    dot_general x20, matrix products, mul_trans(): lax.dot_general(left_side, right_side, (((1,), (1,)), ((), ())), precisio...  101 us
  transfers between devices with their start and end apart: 32, of which 27 were waited for; matrix products, arithmetic and copies ran while one was open for 13% of the time, Pallas kernels for 0%

commit v1 on v0

v1 whole, which is shorter than its diff:
```python
import functools

import jax
import jax.numpy as jnp
from jax import lax
from jax.experimental import pallas as pl
from jax.experimental.pallas import tpu as pltpu
from jax.sharding import PartitionSpec as P

MESH = pl.DeviceIdType.MESH
F32, BF16 = jnp.float32, jnp.bfloat16
LANES = 128
PAR = 32
TALL = 16
CUTS = 2
SLOTS = 3 * CUTS


def schedule(levels):
    sums = [1, 4, 6, 8] + [8 + k for k in range(1, levels - 1)]
    gap = 2 if levels < 4 else 1
    return sums + [sums[-1] + 1 + gap * k for k in range(levels)]


def rings(levels):
    return -(-(schedule(levels)[levels + 2] + 1) // SLOTS), 2


def flip(index, stride):
    return index + stride - 2 * stride * ((index // stride) % 2)


def split(value):
    high = value.astype(BF16)
    return high, (value - high.astype(F32)).astype(BF16)


def dot3(left, right, dims):
    def one(a, b):
        return lax.dot_general(a, b, (dims, ((), ())), preferred_element_type=F32)

    return one(left[0], right[1]) + one(left[1], right[0]) + one(left[0], right[0])


NN, NT, TN = ((1,), (0,)), ((1,), (1,)), ((0,), (0,))


def remote(src, dst, send, recv, device):
    return pltpu.make_async_remote_copy(
        src_ref=src, dst_ref=dst, send_sem=send, recv_sem=recv, device_id=device, device_id_type=MESH
    )


def meet(devices):
    barrier = pltpu.get_barrier_semaphore()
    for device in devices:
        pl.semaphore_signal(barrier, inc=1, device_id=device, device_id_type=MESH)
    pl.semaphore_wait(barrier, len(devices))


def sum_slots(ref):
    total = ref[0]
    for k in range(1, ref.shape[0]):
        total = total + ref[k]
    return total


def merge_stats(ref):
    parts = [ref[k] for k in range(ref.shape[0])]
    count = functools.reduce(jnp.add, [p[0:1] for p in parts])
    sums = functools.reduce(jnp.add, [p[1:2] for p in parts])
    mean = sums / jnp.maximum(count, 1.0)
    square = jnp.zeros_like(sums)
    for p in parts:
        gap = p[1:2] / jnp.maximum(p[0:1], 1.0) - mean
        square = square + (p[2:3] + p[0:1] * gap * gap)
    return jnp.concatenate([count, sums, square, jnp.zeros((5, sums.shape[1]), F32)], axis=0)


def kernel(
    sections, rows, levels, classes,
    feat_ref, wz_ref, wr_ref, wo_ref, whead_ref, count_ref, valid_ref,
    mask_ref, bz_ref, br_ref, bo_ref, gain_ref, shift_ref, bhead_ref, wout_ref, bout_ref, cot_ref,
    gz_out, gr_out, go_out, gfeat_out, ghead_out, logit_out, tiny_out, vec_out, wfull,
    x_buf, small_buf, par, hs, zs, rs, cs, weight, upper,
    whead, x_hat, logit_buf, dh, d_in, d_reset, gin, vec,
    small_ref, wout_buf, dlog_buf, turn,
    grads, core_buf, total, land,
    h_grads, h_core, h_total, h_land,
    ex_a, ex_a_feat, ex_a_rows, ex_b, ex_b_feat, ex_b_rows, ex_c_feat, ex_c_rows,
    first_s, first_r, first_l, fy_s, fy_r, a_s, a_r, x_s, x_r, z_s, z_r, b_s, b_r, c_s, c_r,
    own_s, own_r, far_s, far_r, load_w, logit_s, logit_r, gf_s, gf_r, gf_l,
    ef_s, ef_r, er_s, er_r,
    core_s, core_r, rs_s, rs_r, ag_s, ag_r, out_l, hu_s, hu_r, hu_l,
):
    r, f = lax.axis_index("rows"), lax.axis_index("feat")
    weights = (wz_ref, wr_ref, wo_ref)
    units = 3 * sections
    depth = wz_ref.shape[1]
    mine, width = x_buf.shape
    blocks = small_buf.shape[0]
    half = width // 2
    core, far, both = flip(f, 1), flip(f, 2), flip(flip(f, 1), 2)
    others = (core, far, both)
    rx, rz = flip(r, 1), flip(r, 2)
    quarter = depth // 4
    cut_b, cut_c = 3 * quarter // 8, 3 * quarter // 8 + 5 * quarter // 16
    q = 2 * (r % 2) + (r // 2) % 2
    q_x, q_z, q_d = flip(q, 2), flip(q, 1), flip(flip(q, 1), 2)

    def lanes(index):
        return pl.ds(pl.multiple_of(index * LANES, LANES), LANES)

    def part(start, size):
        return pl.ds(pl.multiple_of(start, 8), size)

    def rows_of(index, start, size):
        return part(index * quarter + start, size)

    meet([(r, peer) for peer in others] + [(lax.rem(r + k, rows), f) for k in range(1, rows)])

    small_ref[...] = jnp.zeros_like(small_ref)
    for k, ref in enumerate((mask_ref, bz_ref, br_ref, bo_ref)):
        small_ref[k * sections : (k + 1) * sections] = ref[...]
    small_ref[4 * sections : 4 * sections + 1] = gain_ref[...]
    small_ref[4 * sections + 1 : 4 * sections + 2] = shift_ref[...]
    own_rows = pl.ds(pl.multiple_of(f * mine, mine), mine)
    firsts, heads = [], []
    for k, peer in enumerate(others):
        chunk = pl.ds(pl.multiple_of(peer * mine, mine), mine)
        firsts += [
            remote(small_ref, small_buf.at[f], first_s.at[k], first_r.at[k], (r, peer)),
            remote(feat_ref.at[chunk], x_buf.at[:, lanes(f)], first_s.at[3 + k], first_r.at[3 + k], (r, peer)),
        ]
        heads.append(remote(whead_ref, whead.at[lanes(f)], first_s.at[6 + k], first_r.at[6 + k], (r, peer)))
    locals_ = [
        pltpu.make_async_copy(small_ref, small_buf.at[f], first_l.at[0]),
        pltpu.make_async_copy(feat_ref.at[own_rows], x_buf.at[:, lanes(f)], first_l.at[1]),
        pltpu.make_async_copy(whead_ref, whead.at[lanes(f)], first_l.at[2]),
    ]

    def y_copy(s, m):
        u, span = 3 * s + m, rows_of(q, 0, quarter)
        return remote(weights[m].at[s, span], wfull.at[s, m, f, span], fy_s.at[u], fy_r.at[u], (r, far))

    def a_copy(s, m):
        u, span = 3 * s + m, rows_of(q_d, 0, cut_b)
        return remote(weights[m].at[s, span], wfull.at[s, m, f, span], a_s.at[u], a_r.at[u], (r, far))

    def own_copy(s, m):
        u = 3 * s + m
        return remote(weights[m].at[s], wfull.at[s, m, f], own_s.at[u], own_r.at[u], (r, core))

    def pass_on(s, m, span, send, recv, device):
        u, ref = 3 * s + m, wfull.at[s, m, far, span]
        return remote(ref, ref, send.at[u], recv.at[u], device)

    def x_copy(s, m):
        return pass_on(s, m, rows_of(q, 0, quarter), x_s, x_r, (rx, f))

    def z_copy(s, m):
        return pass_on(s, m, rows_of(q, 0, quarter), z_s, z_r, (rz, f))

    def b_copy(s, m):
        return pass_on(s, m, rows_of(q_z, cut_b, cut_c - cut_b), b_s, b_r, (rx, f))

    def c_copy(s, m):
        return pass_on(s, m, rows_of(q_x, cut_c, quarter - cut_c), c_s, c_r, (rz, f))

    def far_copy(s, m):
        u, ref = 3 * s + m, wfull.at[s, m, far]
        return remote(ref, ref, far_s.at[u], far_r.at[u], (r, core))

    def w_load(s, m):
        copies = [pltpu.make_async_copy(weights[m].at[s], weight.at[m, :, lanes(f)], load_w.at[m, 0])]
        for k, b in enumerate(others):
            copies.append(
                pltpu.make_async_copy(wfull.at[s, m, b], weight.at[m, :, lanes(b)], load_w.at[m, 1 + k])
            )
        return copies

    def start(copies):
        for copy in copies:
            copy.start()

    def wait(copies):
        for copy in copies:
            copy.wait()

    def send_own(s):
        for m in range(3):
            y_copy(s, m).start()
            a_copy(s, m).start()
            own_copy(s, m).start()

    send_own(0)
    start(firsts + locals_)

    @pl.loop(1, sections)
    def _(s):
        send_own(s)

    start(heads)

    def arrange():
        for copy in firsts:
            copy.wait_recv()
        wait(locals_)
        par[...] = jnp.concatenate([small_buf[b] for b in range(blocks)], axis=1)
        logits = par[0:8]
        probs = jnp.exp(logits - jnp.max(logits, axis=1, keepdims=True))
        probs = probs / jnp.sum(probs, axis=1, keepdims=True)
        par[0:sections] = (width * probs)[0:sections]
        hs[0] = x_buf[...]

    def put(value, at_rows):
        for k, piece in enumerate(split(value)):
            upper[k, :, at_rows] = piece

    low_cols, high_cols = slice(0, width), slice(width, 2 * width)

    def product(s, m):
        tiles = []
        for t in range(2):
            w = split(weight[m, :, t * half : (t + 1) * half])
            tiles.append(dot3((upper[0], upper[1]), w, NN))
        return jnp.concatenate(tiles, axis=1) + par[pl.ds(sections * (m + 1) + s, 1), :]

    def gate(s, m):
        if m == 0:
            put(hs[s], low_cols)
            put(x_buf[...] * par[pl.ds(s, 1), :], high_cols)
            zs[s] = jax.nn.sigmoid(product(s, 0))
        elif m == 1:
            rs[s] = jax.nn.sigmoid(product(s, 1))
            put(rs[s] * hs[s], low_cols)
        else:
            cand = jnp.tanh(product(s, 2))
            cs[s] = cand
            hs[s + 1] = hs[s] + zs[s] * (cand - hs[s])

    def at(step, m, back_by):
        u = m - back_by
        return step + u // 3, u % 3

    @pl.loop(0, sections + 1)
    def _(step):
        for m in range(3):

            @pl.when(step < sections)
            def _():
                y_copy(step, m).wait_recv()
                x_copy(step, m).start()
                z_copy(step, m).start()

            s1, m1 = at(step, m, 1)

            @pl.when((s1 >= 0) & (s1 < sections))
            def _():
                x_copy(s1, m1).wait_recv()
                z_copy(s1, m1).wait_recv()
                b_copy(s1, m1).start()
                c_copy(s1, m1).start()

            s2, m2 = at(step, m, 2)

            @pl.when((s2 >= 0) & (s2 < sections))
            def _():
                a_copy(s2, m2).wait_recv()
                b_copy(s2, m2).wait_recv()
                c_copy(s2, m2).wait_recv()
                far_copy(s2, m2).start()

            if m == 0:
                pl.when(step == 1)(arrange)

            @pl.when(step >= 1)
            def _():
                own_copy(step - 1, m).wait_recv()
                far_copy(step - 1, m).wait_recv()
                copies = w_load(step - 1, m)
                start(copies)
                wait(copies)
                gate(step - 1, m)

    def feat_step(n, src, slots):
        return [
            remote(src, slots.at[f], ef_s.at[n, k], ef_r.at[n, k], (r, peer)) for k, peer in enumerate(others)
        ]

    def rows_step(n, src, slots):
        return [
            remote(src, slots.at[r], er_s.at[n, k - 1], er_r.at[n, k - 1], (lax.rem(r + k, rows), f))
            for k in range(1, rows)
        ]

    def sum_all(n, value, src, feat_slots, row_slots, merge):
        feat_slots[f] = value
        src[...] = value
        copies = feat_step(n, src, feat_slots)
        start(copies)
        wait(copies)
        value = merge(feat_slots)
        row_slots[r] = value
        src[...] = value
        copies = rows_step(n, src, row_slots)
        start(copies)
        return copies

    for m in (2, 0, 1):
        start(w_load(sections - 1, m))
    here = pl.ds(pl.multiple_of(f * mine, mine), mine)
    place = lax.broadcasted_iota(jnp.int32, (1, mine), 1) + f * mine
    flat = jnp.where(place < count_ref[0], 1.0, 0.0) * valid_ref[:, here].astype(F32)
    column = jnp.transpose(jnp.broadcast_to(flat, (8, mine)))[:, 0:1]
    wout_buf[...] = jnp.zeros_like(wout_buf)
    wout_buf[0:classes] = wout_ref[...]
    dlog_buf[...] = jnp.zeros_like(dlog_buf)
    dlog_buf[0:classes] = cot_ref[:, here] * flat
    turn[...] = jnp.zeros_like(turn)
    turn[0:1, 0:classes] = bout_ref[...]
    b_out = jnp.transpose(turn[...])[0:TALL, 0:1]
    current = hs[sections]
    count = jnp.sum(column, axis=0, keepdims=True)
    sums = jnp.sum(column * current, axis=0, keepdims=True)
    gap = current - sums / jnp.maximum(count, 1.0)
    square = jnp.sum(column * gap * gap, axis=0, keepdims=True)
    stats = jnp.concatenate(
        [jnp.broadcast_to(count, sums.shape), sums, square, jnp.zeros((5, width), F32)], axis=0
    )
    wait(sum_all(0, stats, ex_a, ex_a_feat, ex_a_rows, merge_stats))
    stats = merge_stats(ex_a_rows)
    count = stats[0:1]
    inv_std = lax.rsqrt(stats[2:3] / count + 1e-05)
    x_hat[...] = (current - stats[1:2] / count) * inv_std
    gain, shift = par[4 * sections : 4 * sections + 1], par[4 * sections + 1 : 4 * sections + 2]
    normed = split(x_hat[...] * gain + shift)
    for copy in heads:
        copy.wait_recv()
    w_head = split(whead[...])
    act = dot3(normed, w_head, NN) + bhead_ref[...]
    phi = 0.5 * (1.0 + lax.erf(act * 0.7071067811865476))
    hidden = split(act * phi)
    slope = phi + act * (jnp.exp(-0.5 * act * act) * 0.3989422804014327)
    w_out = split(wout_buf[...])
    logit_buf[f] = (dot3(w_out, hidden, NT) + b_out) * flat
    logit_copies = [
        remote(logit_buf.at[f], logit_buf.at[f], logit_s.at[k], logit_r.at[k], (r, peer))
        for k, peer in enumerate(others)
    ]
    start(logit_copies)
    d_log = dlog_buf[...]
    d_act = dot3(split(d_log), w_out, TN) * slope
    d_act2 = split(d_act)
    d_normed = dot3(d_act2, w_head, NT)
    sums = jnp.concatenate(
        [
            jnp.sum(d_normed * x_hat[...], axis=0, keepdims=True),
            jnp.sum(d_normed, axis=0, keepdims=True),
            jnp.zeros((6, width), F32),
        ],
        axis=0,
    )
    dh[...] = d_normed
    copies = sum_all(1, sums, ex_b, ex_b_feat, ex_b_rows, sum_slots)
    vec[...] = jnp.zeros_like(vec)
    hid = act.shape[1]
    aux = 4 * sections
    vec[aux : aux + TALL, 0:hid] = dot3(split(d_log), hidden, NN)
    vec[aux + classes : aux + classes + 1, 0:hid] = jnp.sum(d_act, axis=0, keepdims=True)
    ones = jnp.ones((8, mine), F32)
    vec[aux + classes + 1 : aux + classes + 2, 0:TALL] = dot3(split(ones), split(d_log), NT)[0:1]
    grad = dot3(normed, d_act2, TN)
    for b in range(blocks):
        for t in range(hid // LANES):
            h_grads[b, t * LANES : (t + 1) * LANES] = grad[
                b * LANES : (b + 1) * LANES, t * LANES : (t + 1) * LANES
            ]
    wait(copies)
    sums = sum_slots(ex_b_rows)
    dh[...] = inv_std * (
        dh[...] * gain - column / count * gain * (sums[1:2] + x_hat[...] * sums[0:1])
    )
    tiny_out[...] = sums
    gin[...] = jnp.zeros_like(gin)

    outs = (go_out, gz_out, gr_out)
    which = (2, 0, 1)
    peers = [(flip(r, 2**k), f) for k in range(levels)]
    piece = depth // CUTS
    held, landed = rings(levels)

    class Unit:
        def __init__(self, step, j):
            m, cut = j // CUTS, j % CUTS
            span = pl.ds(cut * piece, piece)
            where = (step % 3) * SLOTS + j
            self.depth = piece
            self.grads = grads.at[(3 * step + m) % 2, :, span]
            self.core, self.total, self.land = core_buf.at[j], total.at[step % held, j], land.at[step % landed, j]
            self.out = outs[m].at[sections - 1 - step, span]
            self.core_sems = [(core_s.at[k, j], core_r.at[k, j]) for k in range(2)]
            self.rs_sems = [(rs_s.at[k, step % landed, j], rs_r.at[k, step % landed, j]) for k in range(levels + 2)]
            self.ag_sems = [(ag_s.at[k, where], ag_r.at[k, where]) for k in range(levels)]
            self.out_sem = out_l.at[where]
            self.plan(["y"] + list(range(levels)) if j < SLOTS - 1 else [1, "y", 0] + list(range(2, levels)))

        def plan(self, order):
            self.moves, self.backs = [], []
            base, size, block_list, landing, sem = 0, self.depth, [0, 1], 0, 0
            for step in order:
                move = []
                if step == "y":
                    device, sent, kept, from_blocks, block_list = (r, far), base, base, [1], [0]
                else:
                    size //= 2
                    side = (r // 2**step) % 2
                    device, sent, kept, from_blocks = (
                        peers[step], base + (1 - side) * size, base + side * size, block_list,
                    )
                    self.backs.append((device, part(kept, size)))
                for k, block in enumerate(from_blocks):
                    move.append(
                        (device, block, part(sent, size), block_list[k], part(kept, size),
                         pl.ds(landing, size), self.rs_sems[sem])
                    )
                    landing += size
                    sem += 1
                self.moves.append(move)
                base = kept
            self.backs.reverse()

        def core_copies(self):
            return [
                remote(self.grads.at[b], self.core.at[k], *self.core_sems[k], (r, core))
                for k, b in enumerate((core, both))
            ]

        def rs_copies(self, i):
            return [
                remote(self.total.at[block, sent], self.land.at[landing], *sems, device)
                for device, block, sent, _, _, landing, sems in self.moves[i]
            ]

        def add(self, i):
            for _, _, _, block, kept, landing, _ in self.moves[i]:
                self.total[block, kept] += self.land[landing]

        def ag_copy(self, i):
            device, kept = self.backs[i]
            dst = self.out.at[kept]
            return remote(self.total.at[0, kept] if i == 0 else dst, dst, *self.ag_sems[i], device)

        def out_local(self):
            kept = self.backs[0][1]
            return pltpu.make_async_copy(self.total.at[0, kept], self.out.at[kept], self.out_sem)

    class HeadUnit(Unit):
        def __init__(self):
            self.depth = h_grads.shape[1]
            self.grads, self.core, self.total, self.land, self.out = h_grads, h_core, h_total, h_land, ghead_out
            sems = [(hu_s.at[k], hu_r.at[k]) for k in range(2 * levels + 4)]
            self.core_sems, self.rs_sems, self.ag_sems = sems[:2], sems[2 : levels + 4], sems[levels + 4 :]
            self.out_sem = hu_l.at[0]
            self.plan(["y"] + list(range(levels)))

    def stage_core(unit):
        wait(unit.core_copies())
        unit.total[1] = unit.grads[far] + unit.core[1]
        unit.total[0] = unit.grads[f] + unit.core[0]
        start(unit.rs_copies(0))

    def stage_sum(i, unit):
        wait(unit.rs_copies(i))
        unit.add(i)
        if i < levels:
            start(unit.rs_copies(i + 1))
        else:
            unit.ag_copy(0).start()
            unit.out_local().start()

    def stage_out(i, unit):
        if i == 0:
            unit.out_local().wait()
        unit.ag_copy(i).wait()
        if i + 1 < levels:
            unit.ag_copy(i + 1).start()

    stages = [stage_core]
    stages += [functools.partial(stage_sum, i) for i in range(levels + 1)]
    stages += [functools.partial(stage_out, i) for i in range(levels)]

    def outer(m, u, right):
        for t in range(2):
            tile = split(right[:, t * half : (t + 1) * half])
            tile = dot3((upper[0], upper[1]), tile, TN)
            for b in range(half // LANES):
                grads[u % 2, t * (half // LANES) + b] = tile[:, b * LANES : (b + 1) * LANES]

    def back(m, left, t):
        return dot3(left, split(weight[which[m], t * half : (t + 1) * half, :]), NT)

    def compute(step, m):
        s = sections - 1 - step
        u = 3 * step + m
        wait(w_load(s, which[m]))
        h = hs[s]
        if m == 0:
            z, reset, c = zs[s], rs[s], cs[s]
            put(reset * h, low_cols)
            put(x_buf[...] * par[pl.ds(s, 1), :], high_cols)
            d_out = dh[...] * z * (1.0 - c * c)
            vec[pl.ds(2 * sections + s, 1), :] = jnp.sum(d_out, axis=0, keepdims=True)
            outer(m, u, d_out)
            left = split(d_out)
            for t in range(4):
                d_in[:, t * half : (t + 1) * half] = back(m, left, t)
            d_reset[...] = d_in[:, 0:width] * h * reset * (1.0 - reset)
        elif m == 1:
            z, reset, c = zs[s], rs[s], cs[s]
            put(h, low_cols)
            d_up = dh[...] * (c - h) * z * (1.0 - z)
            vec[pl.ds(s, 1), :] = jnp.sum(d_up, axis=0, keepdims=True)
            outer(m, u, d_up)
            dh[...] = dh[...] * (1.0 - z) + d_in[:, 0:width] * reset
            left = split(d_up)
            for t in range(4):
                cols = slice(t % 2 * half, (t % 2 + 1) * half)
                if t < 2:
                    dh[:, cols] += back(m, left, t)
                else:
                    d_in[:, t * half : (t + 1) * half] += back(m, left, t)
        else:
            d_r = d_reset[...]
            vec[pl.ds(sections + s, 1), :] = jnp.sum(d_r, axis=0, keepdims=True)
            outer(m, u, d_r)
            left = split(d_r)
            for t in range(4):
                cols = slice(t % 2 * half, (t % 2 + 1) * half)
                if t < 2:
                    dh[:, cols] += back(m, left, t)
                else:
                    d_xs = d_in[:, t * half : (t + 1) * half] + back(m, left, t)
                    gin[:, cols] += d_xs * par[pl.ds(s, 1), cols]
                    vec[pl.ds(3 * sections + s, 1), cols] = jnp.sum(d_xs * x_buf[:, cols], axis=0, keepdims=True)

        @pl.when(step + 1 < sections)
        def _():
            start(w_load(s - 1, which[m]))

    gf_copies = [
        remote(gin.at[:, lanes(peer)], gfeat_out.at[own_rows], gf_s.at[k], gf_r.at[k], (r, peer))
        for k, peer in enumerate(others)
    ]
    gf_local = pltpu.make_async_copy(gin.at[:, lanes(f)], gfeat_out.at[own_rows], gf_l.at[0])
    vec_feat = feat_step(2, vec, ex_c_feat)
    vec_rows = rows_step(2, vec, ex_c_rows)

    start(HeadUnit().core_copies())

    def before(step, j, back_by):
        u = j - back_by
        return step + u // SLOTS, u % SLOTS

    delays = schedule(levels)

    @pl.loop(0, sections + -(-delays[-1] // SLOTS))
    def _(step):
        for j in range(SLOTS):

            @pl.when(step < sections)
            def _():
                if j % CUTS == 0:
                    compute(step, j // CUTS)
                start(Unit(step, j).core_copies())

            for delay, stage in zip(delays, stages, strict=True):
                s1, j1 = before(step, j, delay)
                if j1 == SLOTS - 1:

                    @pl.when(s1 == -1)
                    def _():
                        stage(HeadUnit())

                @pl.when((s1 >= 0) & (s1 < sections))
                def _():
                    stage(Unit(s1, j1))

            if j == 0:

                @pl.when(step == sections)
                def _():
                    ex_c_feat[f] = vec[...]
                    start(vec_feat)
                    gin[...] += dh[...]
                    start(gf_copies + [gf_local])

            if j == 2:

                @pl.when(step == sections)
                def _():
                    wait(vec_feat)
                    vec[...] = sum_slots(ex_c_feat)
                    ex_c_rows[r] = vec[...]
                    start(vec_rows)

    wait(vec_rows)
    sums = sum_slots(ex_c_rows)
    scale, gsc = par[0:sections], sums[3 * sections : 4 * sections]
    vec_out[...] = sums
    vec_out[3 * sections : 4 * sections] = scale * (gsc - jnp.sum(scale * gsc, axis=1, keepdims=True) / width)
    wait(gf_copies + [gf_local])
    wait(logit_copies)
    for b in range(blocks):
        logit_out[:, b * mine : (b + 1) * mine] = logit_buf[b]

    @pl.loop(0, sections)
    def _(s):
        for m in range(3):
            for copy in (y_copy, a_copy, own_copy, x_copy, z_copy, b_copy, c_copy, far_copy):
                copy(s, m).wait_send()

    for copy in firsts + heads:
        copy.wait_send()


def finish_kernel(
    sections, classes,
    gz_ref, gr_ref, go_ref, gfeat_ref, ghead_ref, logit_ref, tiny_ref, vec_ref,
    logit_out, gfeat_out, gmask_out, gz_out, gr_out, go_out, bz_out, br_out, bo_out,
    gain_out, shift_out, ghead_out, bhead_out, wout_out, bout_out,
    big, feat, head, load, store,
):
    f = lax.axis_index("feat")
    pairs = [(feat, gfeat_ref, gfeat_out)] + [
        (big.at[m, s], src.at[s], dst.at[s])
        for s in range(sections)
        for m, (src, dst) in enumerate(((gz_ref, gz_out), (gr_ref, gr_out), (go_ref, go_out)))
    ]
    loads = [pltpu.make_async_copy(src, held, load.at[k]) for k, (held, src, _) in enumerate(pairs)]
    stores = [pltpu.make_async_copy(held, dst, store.at[k]) for k, (held, _, dst) in enumerate(pairs)]
    for copy in loads:
        copy.start()
    block = feat.shape[1]
    cols = pl.ds(pl.multiple_of(f * block, block), block)
    hidden = bhead_out.shape[1]
    aux = 4 * sections
    logit_out[...] = logit_ref[0:classes]
    for k, out in enumerate((bz_out, br_out, bo_out, gmask_out)):
        out[...] = vec_ref[k * sections : (k + 1) * sections, cols]
    gain_out[...] = tiny_ref[0:1, cols]
    shift_out[...] = tiny_ref[1:2, cols]
    for t in range(hidden // block):
        ghead_out[:, t * block : (t + 1) * block] = ghead_ref[t * block : (t + 1) * block]
    wout_out[...] = vec_ref[aux : aux + classes, 0:hidden]
    bhead_out[...] = vec_ref[aux + classes : aux + classes + 1, 0:hidden]
    bout_out[...] = vec_ref[aux + classes + 1 : aux + classes + 2, 0:classes]
    for load_, store_ in zip(loads, stores, strict=True):
        load_.wait()
        store_.start()
    for copy in stores:
        copy.wait()


def layer(
    rows, groups, features, w_update, w_reset, w_candidate, w_head, counts, validity, mask_logits, b_update, b_reset,
    b_candidate, norm_gain, norm_shift, b_head, w_out, b_out, cotangent,
):
    sections, depth, block = w_update.shape
    width, mine = groups * block, features.shape[0] // groups
    hidden = w_head.shape[1]
    classes = w_out.shape[0]
    units = 3 * sections
    levels = rows.bit_length() - 1
    head_depth = max(hidden, 8 * rows)
    piece = depth // CUTS
    held, landed = rings(levels)
    long = 4 * sections + TALL
    sds = jax.ShapeDtypeStruct
    dma = pltpu.SemaphoreType.DMA
    any_, vmem = pl.BlockSpec(memory_space=pl.ANY), pl.BlockSpec(memory_space=pltpu.VMEM)
    grad = sds((sections, depth, block), F32)

    def buf(*shape):
        return pltpu.VMEM(shape, F32)

    made = pl.pallas_call(
        functools.partial(kernel, sections, rows, levels, classes),
        out_shape=[
            grad, grad, grad,
            sds(features.shape, F32),
            sds((head_depth, block), F32),
            sds((TALL, groups * mine), F32),
            sds((8, width), F32),
            sds((long, width), F32),
            sds((sections, 3, groups, depth, block), F32),
        ],
        in_specs=[any_] * 5 + [pl.BlockSpec(memory_space=pltpu.SMEM)] + [vmem] * 11,
        out_specs=[any_] * 5 + [vmem] * 3 + [any_],
        scratch_shapes=[
            buf(mine, width), buf(groups, PAR, block), buf(PAR, width), buf(sections + 1, mine, width),
            buf(sections, mine, width), buf(sections, mine, width), buf(sections, mine, width),
            buf(3, depth, width), pltpu.VMEM((2, mine, depth), BF16),
            buf(width, hidden), buf(mine, width), buf(groups, TALL, mine), buf(mine, width),
            buf(mine, depth), buf(mine, width), buf(mine, width), buf(long, width),
            buf(PAR, block), buf(TALL, hidden), buf(TALL, mine), buf(8, LANES),
            buf(2, groups, depth, block), buf(SLOTS, 2, piece, block), buf(held, SLOTS, 2, piece, block),
            buf(landed, SLOTS, 2 * piece, block),
            buf(groups, head_depth, block), buf(2, head_depth, block), buf(2, head_depth, block),
            buf(2 * head_depth, block),
            buf(8, width), buf(groups, 8, width), buf(rows, 8, width),
            buf(8, width), buf(groups, 8, width), buf(rows, 8, width),
            buf(groups, long, width), buf(rows, long, width),
            dma((9,)), dma((9,)), dma((3,)),
        ] + [dma((units,))] * 16 + [
            dma((3, groups)), dma((3,)), dma((3,)), dma((3,)), dma((3,)), dma((1,)),
            dma((3, 3)), dma((3, 3)), dma((3, rows - 1)), dma((3, rows - 1)),
            dma((2, SLOTS)), dma((2, SLOTS)), dma((levels + 2, landed, SLOTS)), dma((levels + 2, landed, SLOTS)),
            dma((levels, 3 * SLOTS)), dma((levels, 3 * SLOTS)), dma((3 * SLOTS,)),
            dma((2 * levels + 4,)), dma((2 * levels + 4,)), dma((1,)),
        ],
        compiler_params=pltpu.CompilerParams(
            collective_id=0, has_side_effects=True, vmem_limit_bytes=62 * 2**20
        ),
    )(
        features, w_update, w_reset, w_candidate, w_head, counts, validity[None], mask_logits, b_update, b_reset,
        b_candidate, norm_gain[None], norm_shift[None], b_head[None], w_out, b_out[None], cotangent,
    )
    row = sds((1, block), F32)
    bias = sds((sections, block), F32)
    return pl.pallas_call(
        functools.partial(finish_kernel, sections, classes),
        out_shape=[
            sds((classes, groups * mine), F32), sds(features.shape, F32), bias, grad, grad, grad, bias, bias, bias,
            row, row, sds((block, hidden), F32), sds((1, hidden), F32), sds((classes, hidden), F32),
            sds((1, classes), F32),
        ],
        in_specs=[any_] * 4 + [vmem] * 4,
        out_specs=[vmem, any_, vmem, any_, any_, any_] + [vmem] * 9,
        scratch_shapes=[
            buf(3, sections, depth, block), buf(*features.shape), buf(8, LANES),
            dma((units + 1,)), dma((units + 1,)),
        ],
        compiler_params=pltpu.CompilerParams(vmem_limit_bytes=62 * 2**20),
    )(*made[:8])


def local(
    rows, groups, features, counts, validity, mask_logits, w_update, w_reset, w_candidate, b_update, b_reset,
    b_candidate, norm_gain, norm_shift, w_head, b_head, w_out, b_out, cotangent,
):
    out = layer(
        rows, groups, features, w_update, w_reset, w_candidate, w_head, counts, validity, mask_logits, b_update,
        b_reset, b_candidate, norm_gain, norm_shift, b_head, w_out.T, b_out, cotangent.T,
    )
    logits, g_feat, g_mask, gz, gr, go, bz, br, bo, gain, shift, g_head, g_b_head, g_w_out, g_b_out = out
    return (
        logits.T, g_feat, g_mask, gz, gr, go, bz, br, bo, gain[0], shift[0], g_head, g_b_head[0], g_w_out.T,
        g_b_out[0],
    )


def solution(mesh):
    rows, groups = mesh.shape["rows"], mesh.shape["feat"]
    split_cols, by_feat = P(None, None, "feat"), P("feat")
    return jax.shard_map(
        functools.partial(local, rows, groups),
        mesh=mesh,
        in_specs=(
            P("rows", "feat"), P("rows"), P("rows"), P(None, "feat"), split_cols, split_cols, split_cols,
            P(None, "feat"), P(None, "feat"), P(None, "feat"), by_feat, by_feat, P("feat", None),
            P(), P(), P(), P("rows", None),
        ),
        out_specs=(
            P("rows", None), P("rows", "feat"), P(None, "feat"), split_cols, split_cols, split_cols,
            P(None, "feat"), P(None, "feat"), P(None, "feat"), by_feat, by_feat, P("feat", None),
            P(), P(), P(),
        ),
        check_vma=False,
    )
```

time: 1560 us -> 383 us (0.25)
  waiting for transfers between devices: 946 us -> 0 us
  Pallas kernels: 0 us -> 381 us
  matrix products: 353 us -> 0 us
  blocking collectives: 111 us -> 0 us
  other arithmetic: 69.4 us -> 0 us
  local copies, waits for them, and re-layouts: 45.1 us -> 0 us
    pallas_call x0 -> x2, Pallas kernels: none -> 381 us  [the longest x1 371 us: layer(): pl.pallas_call(functools.partial(kernel, sections, rows, levels, classes)...]
    dot_general x60 -> x0, matrix products: 353 us -> none  [the longest x20 142 us: trans_mul(): lax.dot_general(left_side, right_side, (((0,), (0,)), ((), ())), precisio...]
    reduce_scatter x18 -> x0, waiting for transfers between devices: 347 us -> none  [the longest x6 157 us: local(): lax.psum_scatter(dupper[:, :width], 'feat', scatter_dimension=1, tiled=True)]
    psum x2 -> x0, waiting for transfers between devices: 326 us -> none  [the longest x1 293 us: local(): lax.psum((jnp.stack(list_wz), jnp.stack(list_wr), jnp.stack(list_wo), jnp...]
    all_gather x12 -> x0, waiting for transfers between devices: 269 us -> none  [the longest x6 136 us: local(): r_all = lax.all_gather(resets * current, 'feat', axis=1, tiled=True)]
    psum x5 -> x0, blocking collectives: 105 us -> none  [the longest x1 38 us: local(): lax.psum((jnp.stack(list_wz), jnp.stack(list_wr), jnp.stack(list_wo), jnp...]
    reduce_sum x22 -> x0, other arithmetic: 36.3 us -> none  [the longest x6 17.5 us: local(): list_bo[section_num] = jnp.sum(d_cand, 0)]
    unnamed x220 -> x0, local copies, waits for them, and re-layouts: 34.9 us -> none
  transfers between devices with their start and end apart: 32 -> 0, of which waited for: 27 -> 0; matrix products, arithmetic and copies ran while one was open for 13% -> 0% of each run, Pallas kernels for 0% -> 0%
where the time goes in v1:
time: 383 us; the launch traced here: 382 us
  Pallas kernels  381 us (99%)
    pallas_call x1, Pallas kernels, layer(): pl.pallas_call(functools.partial(kernel, sections, rows, levels, classes)...  371 us
    pallas_call x1, Pallas kernels, layer(): pl.pallas_call(functools.partial(finish_kernel, sections, classes), out_s...  9.56 us

profile of v1, /device:TPU:0, one launch (start us, length us, event | category | flops | bytes accessed | tf_op | source)
XLA Modules:
  0.0 382.3 jit_solution(6410640707014925176)
XLA Ops:
  1.3 371.4 %shard_map.280 = (f32[6,1024,128]{2,1,0:T(8,128)}, f32[6,1024,128]{2,1,0:T(8,128)}, f32[6,1024,128]{2,1,0:T(8,128)}, f32[1024,128]{1,0:T(8,128)}, f32[256,128]{1...) custom-call(f32[1024,128]{1,0:T(8,128)} %feat_ref.1, ...), custom_call_target="tpu_custom_call" | custom-call | tf_op jit(solution)/shard_map/pallas_call | solution.py:687
  372.7 9.6 %shard_map.281 = (f32[10,1024]{1,0:T(8,128)}, f32[1024,128]{1,0:T(8,128)}, f32[6,128]{1,0:T(8,128)}, f32[6,1024,128]{2,1,0:T(8,128)}, f32[6,1024,128]{2,1,0:T(8,...) custom-call(f32[6,1024,128]{2,1,0:T(8,128)} %get-tuple-element.38.gz, ...), custom_call_target="tpu_custom_call" | custom-call | tf_op jit(solution)/shard_map/pallas_call | solution.py:731

commit v2 on v1

--- a/solution.py
+++ b/solution.py
@@ -12,18 +12,26 @@
 LANES = 128
 PAR = 32
 TALL = 16
-CUTS = 2
-SLOTS = 3 * CUTS
+
+
+def cuts_of(levels):
+    return 4 if levels < 6 else 2
+
+
+def early(levels):
+    return ((0, 3, 4, 7, 10), (2, 8), (3, 8)) if levels < 6 else ((5,),) * 3
 
 
 def schedule(levels):
-    sums = [1, 4, 6, 8] + [8 + k for k in range(1, levels - 1)]
+    if levels == 3:
+        return [1, 4, 7, 9, 11, 13, 15, 18]
+    sums = [1, 4, 7, 9] + [9 + k for k in range(1, levels - 1)]
     gap = 2 if levels < 4 else 1
     return sums + [sums[-1] + 1 + gap * k for k in range(levels)]
 
 
 def rings(levels):
-    return -(-(schedule(levels)[levels + 2] + 1) // SLOTS), 2
+    return -(-(schedule(levels)[levels + 2] + 1) // (3 * cuts_of(levels))), 2
 
 
 def flip(index, stride):
@@ -65,29 +73,40 @@
     return total
 
 
-def merge_stats(ref):
+def merge_stats(blocks, ref):
     parts = [ref[k] for k in range(ref.shape[0])]
-    count = functools.reduce(jnp.add, [p[0:1] for p in parts])
-    sums = functools.reduce(jnp.add, [p[1:2] for p in parts])
+    counts = [p[2 * blocks : 2 * blocks + 1] for p in parts]
+    count = functools.reduce(jnp.add, counts)
+    sums = functools.reduce(jnp.add, [p[0:blocks] for p in parts])
     mean = sums / jnp.maximum(count, 1.0)
     square = jnp.zeros_like(sums)
-    for p in parts:
-        gap = p[1:2] / jnp.maximum(p[0:1], 1.0) - mean
-        square = square + (p[2:3] + p[0:1] * gap * gap)
-    return jnp.concatenate([count, sums, square, jnp.zeros((5, sums.shape[1]), F32)], axis=0)
+    for p, n in zip(parts, counts, strict=True):
+        gap = p[0:blocks] / jnp.maximum(n, 1.0) - mean
+        square = square + (p[blocks : 2 * blocks] + n * gap * gap)
+    rest = ref.shape[1] - 2 * blocks - 1
+    return jnp.concatenate([sums, square, count, jnp.zeros((rest, LANES), F32)], axis=0)
+
+
+def stack(row):
+    return [row[:, k * LANES : (k + 1) * LANES] for k in range(row.shape[1] // LANES)]
+
+
+def unstack(value):
+    return jnp.concatenate([value[k : k + 1] for k in range(value.shape[0])], axis=1)
 
 
 def kernel(
     sections, rows, levels, classes,
     feat_ref, wz_ref, wr_ref, wo_ref, whead_ref, count_ref, valid_ref,
     mask_ref, bz_ref, br_ref, bo_ref, gain_ref, shift_ref, bhead_ref, wout_ref, bout_ref, cot_ref,
-    gz_out, gr_out, go_out, gfeat_out, ghead_out, logit_out, tiny_out, vec_out, wfull,
+    gz_out, gr_out, go_out, gfeat_out, ghead_out, logit_out, tiny_out, own_out, aux_out, wfull,
     x_buf, small_buf, par, hs, zs, rs, cs, weight, upper,
     whead, x_hat, logit_buf, dh, d_in, d_reset, gin, vec,
     small_ref, wout_buf, dlog_buf, turn,
     grads, core_buf, total, land,
     h_grads, h_core, h_total, h_land,
-    ex_a, ex_a_feat, ex_a_rows, ex_b, ex_b_feat, ex_b_rows, ex_c_feat, ex_c_rows,
+    ex_a, ex_a_feat, ex_a_rows, ex_b, ex_b_feat, ex_b_rows,
+    ex_c, ex_c_feat, ex_c_mid, ex_c_rows, ex_d, ex_d_feat,
     first_s, first_r, first_l, fy_s, fy_r, a_s, a_r, x_s, x_r, z_s, z_r, b_s, b_r, c_s, c_r,
     own_s, own_r, far_s, far_r, load_w, logit_s, logit_r, gf_s, gf_r, gf_l,
     ef_s, ef_r, er_s, er_r,
@@ -97,6 +116,8 @@
     weights = (wz_ref, wr_ref, wo_ref)
     units = 3 * sections
     depth = wz_ref.shape[1]
+    cuts = cuts_of(levels)
+    slots = 3 * cuts
     mine, width = x_buf.shape
     blocks = small_buf.shape[0]
     half = width // 2
@@ -243,7 +264,7 @@
         u = m - back_by
         return step + u // 3, u % 3
 
-    @pl.loop(0, sections + 1)
+    @pl.loop(0, sections + 2)
     def _(step):
         for m in range(3):
 
@@ -271,17 +292,22 @@
                 c_copy(s2, m2).wait_recv()
                 far_copy(s2, m2).start()
 
+            s3, m3 = at(step, m, 3)
+
+            @pl.when((s3 >= 0) & (s3 < sections))
+            def _():
+                own_copy(s3, m3).wait_recv()
+                far_copy(s3, m3).wait_recv()
+                start(w_load(s3, m3))
+
             if m == 0:
                 pl.when(step == 1)(arrange)
-
-            @pl.when(step >= 1)
+            s4, m4 = at(step, m, 4)
+
+            @pl.when((s4 >= 0) & (s4 < sections))
             def _():
-                own_copy(step - 1, m).wait_recv()
-                far_copy(step - 1, m).wait_recv()
-                copies = w_load(step - 1, m)
-                start(copies)
-                wait(copies)
-                gate(step - 1, m)
+                wait(w_load(s4, m4))
+                gate(s4, m4)
 
     def feat_step(n, src, slots):
         return [
@@ -325,14 +351,14 @@
     sums = jnp.sum(column * current, axis=0, keepdims=True)
     gap = current - sums / jnp.maximum(count, 1.0)
     square = jnp.sum(column * gap * gap, axis=0, keepdims=True)
-    stats = jnp.concatenate(
-        [jnp.broadcast_to(count, sums.shape), sums, square, jnp.zeros((5, width), F32)], axis=0
-    )
-    wait(sum_all(0, stats, ex_a, ex_a_feat, ex_a_rows, merge_stats))
-    stats = merge_stats(ex_a_rows)
-    count = stats[0:1]
-    inv_std = lax.rsqrt(stats[2:3] / count + 1e-05)
-    x_hat[...] = (current - stats[1:2] / count) * inv_std
+    rest = jnp.zeros((ex_a.shape[0] - 2 * blocks - 1, LANES), F32)
+    stats = jnp.concatenate(stack(sums) + stack(square) + [jnp.broadcast_to(count, (1, LANES)), rest], axis=0)
+    merge = functools.partial(merge_stats, blocks)
+    wait(sum_all(0, stats, ex_a, ex_a_feat, ex_a_rows, merge))
+    stats = merge(ex_a_rows)
+    count = stats[2 * blocks : 2 * blocks + 1, 0:1]
+    inv_std = lax.rsqrt(unstack(stats[blocks : 2 * blocks]) / count + 1e-05)
+    x_hat[...] = (current - unstack(stats[0:blocks]) / count) * inv_std
     gain, shift = par[4 * sections : 4 * sections + 1], par[4 * sections + 1 : 4 * sections + 2]
     normed = split(x_hat[...] * gain + shift)
     for copy in heads:
@@ -354,11 +380,8 @@
     d_act2 = split(d_act)
     d_normed = dot3(d_act2, w_head, NT)
     sums = jnp.concatenate(
-        [
-            jnp.sum(d_normed * x_hat[...], axis=0, keepdims=True),
-            jnp.sum(d_normed, axis=0, keepdims=True),
-            jnp.zeros((6, width), F32),
-        ],
+        stack(jnp.sum(d_normed * x_hat[...], axis=0, keepdims=True))
+        + stack(jnp.sum(d_normed, axis=0, keepdims=True)),
         axis=0,
     )
     dh[...] = d_normed
@@ -378,23 +401,23 @@
             ]
     wait(copies)
     sums = sum_slots(ex_b_rows)
-    dh[...] = inv_std * (
-        dh[...] * gain - column / count * gain * (sums[1:2] + x_hat[...] * sums[0:1])
-    )
+    g_gain, g_shift = unstack(sums[0:blocks]), unstack(sums[blocks:])
+    dh[...] = inv_std * (dh[...] * gain - column / count * gain * (g_shift + x_hat[...] * g_gain))
     tiny_out[...] = sums
     gin[...] = jnp.zeros_like(gin)
 
     outs = (go_out, gz_out, gr_out)
     which = (2, 0, 1)
     peers = [(flip(r, 2**k), f) for k in range(levels)]
-    piece = depth // CUTS
+    piece = depth // cuts
     held, landed = rings(levels)
+    z_first = early(levels)
 
     class Unit:
-        def __init__(self, step, j):
-            m, cut = j // CUTS, j % CUTS
+        def __init__(self, step, j, by_z=False):
+            m, cut = j // cuts, j % cuts
             span = pl.ds(cut * piece, piece)
-            where = (step % 3) * SLOTS + j
+            where = (step % 3) * slots + j
             self.depth = piece
             self.grads = grads.at[(3 * step + m) % 2, :, span]
             self.core, self.total, self.land = core_buf.at[j], total.at[step % held, j], land.at[step % landed, j]
@@ -403,7 +426,7 @@
             self.rs_sems = [(rs_s.at[k, step % landed, j], rs_r.at[k, step % landed, j]) for k in range(levels + 2)]
             self.ag_sems = [(ag_s.at[k, where], ag_r.at[k, where]) for k in range(levels)]
             self.out_sem = out_l.at[where]
-            self.plan(["y"] + list(range(levels)) if j < SLOTS - 1 else [1, "y", 0] + list(range(2, levels)))
+            self.plan([1, "y", 0] + list(range(2, levels)) if by_z else ["y"] + list(range(levels)))
 
         def plan(self, order):
             self.moves, self.backs = [], []
@@ -553,44 +576,59 @@
         for k, peer in enumerate(others)
     ]
     gf_local = pltpu.make_async_copy(gin.at[:, lanes(f)], gfeat_out.at[own_rows], gf_l.at[0])
-    vec_feat = feat_step(2, vec, ex_c_feat)
-    vec_rows = rows_step(2, vec, ex_c_rows)
+    vec_feat = [
+        remote(ex_c.at[peer], ex_c_feat.at[f], ef_s.at[2, k], ef_r.at[2, k], (r, peer)) for k, peer in enumerate(others)
+    ]
+    vec_rows = rows_step(2, ex_c_mid, ex_c_rows)
+    vec_last = feat_step(3, ex_d, ex_d_feat)
+    spread = hid // LANES
 
     start(HeadUnit().core_copies())
 
     def before(step, j, back_by):
         u = j - back_by
-        return step + u // SLOTS, u % SLOTS
+        return step + u // slots, u % slots
 
     delays = schedule(levels)
 
-    @pl.loop(0, sections + -(-delays[-1] // SLOTS))
+    @pl.loop(0, sections + -(-delays[-1] // slots))
     def _(step):
-        for j in range(SLOTS):
+        for j in range(slots):
 
             @pl.when(step < sections)
             def _():
-                if j % CUTS == 0:
-                    compute(step, j // CUTS)
+                if j % cuts == 0:
+                    compute(step, j // cuts)
                 start(Unit(step, j).core_copies())
 
             for delay, stage in zip(delays, stages, strict=True):
                 s1, j1 = before(step, j, delay)
-                if j1 == SLOTS - 1:
+                if j1 == slots - 1:
 
                     @pl.when(s1 == -1)
                     def _():
                         stage(HeadUnit())
 
-                @pl.when((s1 >= 0) & (s1 < sections))
-                def _():
-                    stage(Unit(s1, j1))
+                groups = (s1 == 0, (s1 > 0) & (s1 < sections - 1), s1 == sections - 1)
+                for by_z in (False, True):
+                    active = [g for g, early_units in zip(groups, z_first, strict=True) if (j1 in early_units) == by_z]
+                    if active:
+
+                        @pl.when(functools.reduce(jnp.logical_or, active))
+                        def _():
+                            stage(Unit(s1, j1, by_z))
 
             if j == 0:
 
                 @pl.when(step == sections)
                 def _():
-                    ex_c_feat[f] = vec[...]
+                    for b in range(blocks):
+                        ex_c[b, 0:aux] = vec[0:aux, b * LANES : (b + 1) * LANES]
+                        ex_c[b, aux : aux + 8] = vec[
+                            aux + 8 * (b // spread) : aux + 8 * (b // spread + 1),
+                            LANES * (b % spread) : LANES * (b % spread + 1),
+                        ]
+                    ex_c_feat[f] = ex_c[f]
                     start(vec_feat)
                     gin[...] += dh[...]
                     start(gf_copies + [gf_local])
@@ -600,15 +638,32 @@
                 @pl.when(step == sections)
                 def _():
                     wait(vec_feat)
-                    vec[...] = sum_slots(ex_c_feat)
-                    ex_c_rows[r] = vec[...]
+                    ex_c_mid[...] = sum_slots(ex_c_feat)
+                    ex_c_rows[r] = ex_c_mid[...]
                     start(vec_rows)
 
-    wait(vec_rows)
-    sums = sum_slots(ex_c_rows)
-    scale, gsc = par[0:sections], sums[3 * sections : 4 * sections]
-    vec_out[...] = sums
-    vec_out[3 * sections : 4 * sections] = scale * (gsc - jnp.sum(scale * gsc, axis=1, keepdims=True) / width)
+            if j == 5:
+
+                @pl.when(step == sections)
+                def _():
+                    wait(vec_rows)
+                    sums = sum_slots(ex_c_rows)
+                    own_out[...] = sums[0:aux]
+                    scale = par[0:sections, lanes(f)]
+                    inner = jnp.sum(scale * sums[3 * sections : aux], axis=1, keepdims=True) / width
+                    ex_d[...] = jnp.zeros_like(ex_d)
+                    ex_d[0:sections] = jnp.broadcast_to(inner, (sections, LANES))
+                    ex_d[8:16] = sums[aux : aux + 8]
+                    ex_d_feat[f] = ex_d[...]
+                    start(vec_last)
+
+    wait(vec_last)
+    inner = sum_slots(ex_d_feat)[0:sections]
+    own_out[3 * sections : aux] = par[0:sections, lanes(f)] * (own_out[3 * sections : aux] - inner)
+    for b in range(blocks):
+        aux_out[8 * (b // spread) : 8 * (b // spread + 1), LANES * (b % spread) : LANES * (b % spread + 1)] = (
+            ex_d_feat[b, 8:16]
+        )
     wait(gf_copies + [gf_local])
     wait(logit_copies)
     for b in range(blocks):
@@ -626,7 +681,7 @@
 
 def finish_kernel(
     sections, classes,
-    gz_ref, gr_ref, go_ref, gfeat_ref, ghead_ref, logit_ref, tiny_ref, vec_ref,
+    gz_ref, gr_ref, go_ref, gfeat_ref, ghead_ref, logit_ref, tiny_ref, own_ref, aux_ref,
     logit_out, gfeat_out, gmask_out, gz_out, gr_out, go_out, bz_out, br_out, bo_out,
     gain_out, shift_out, ghead_out, bhead_out, wout_out, bout_out,
     big, feat, head, load, store,
@@ -642,19 +697,17 @@
     for copy in loads:
         copy.start()
     block = feat.shape[1]
-    cols = pl.ds(pl.multiple_of(f * block, block), block)
     hidden = bhead_out.shape[1]
-    aux = 4 * sections
     logit_out[...] = logit_ref[0:classes]
     for k, out in enumerate((bz_out, br_out, bo_out, gmask_out)):
-        out[...] = vec_ref[k * sections : (k + 1) * sections, cols]
-    gain_out[...] = tiny_ref[0:1, cols]
-    shift_out[...] = tiny_ref[1:2, cols]
+        out[...] = own_ref[k * sections : (k + 1) * sections]
+    gain_out[...] = tiny_ref[pl.ds(f, 1)]
+    shift_out[...] = tiny_ref[pl.ds(tiny_ref.shape[0] // 2 + f, 1)]
     for t in range(hidden // block):
         ghead_out[:, t * block : (t + 1) * block] = ghead_ref[t * block : (t + 1) * block]
-    wout_out[...] = vec_ref[aux : aux + classes, 0:hidden]
-    bhead_out[...] = vec_ref[aux + classes : aux + classes + 1, 0:hidden]
-    bout_out[...] = vec_ref[aux + classes + 1 : aux + classes + 2, 0:classes]
+    wout_out[...] = aux_ref[0:classes]
+    bhead_out[...] = aux_ref[classes : classes + 1]
+    bout_out[...] = aux_ref[classes + 1 : classes + 2, 0:classes]
     for load_, store_ in zip(loads, stores, strict=True):
         load_.wait()
         store_.start()
@@ -673,7 +726,9 @@
     units = 3 * sections
     levels = rows.bit_length() - 1
     head_depth = max(hidden, 8 * rows)
-    piece = depth // CUTS
+    cuts = cuts_of(levels)
+    slots = 3 * cuts
+    piece = depth // cuts
     held, landed = rings(levels)
     long = 4 * sections + TALL
     sds = jax.ShapeDtypeStruct
@@ -691,12 +746,13 @@
             sds(features.shape, F32),
             sds((head_depth, block), F32),
             sds((TALL, groups * mine), F32),
-            sds((8, width), F32),
-            sds((long, width), F32),
+            sds((2 * groups, block), F32),
+            sds((4 * sections, block), F32),
+            sds((TALL, hidden), F32),
             sds((sections, 3, groups, depth, block), F32),
         ],
         in_specs=[any_] * 5 + [pl.BlockSpec(memory_space=pltpu.SMEM)] + [vmem] * 11,
-        out_specs=[any_] * 5 + [vmem] * 3 + [any_],
+        out_specs=[any_] * 5 + [vmem] * 4 + [any_],
         scratch_shapes=[
             buf(mine, width), buf(groups, PAR, block), buf(PAR, width), buf(sections + 1, mine, width),
             buf(sections, mine, width), buf(sections, mine, width), buf(sections, mine, width),
@@ -704,19 +760,20 @@
             buf(width, hidden), buf(mine, width), buf(groups, TALL, mine), buf(mine, width),
             buf(mine, depth), buf(mine, width), buf(mine, width), buf(long, width),
             buf(PAR, block), buf(TALL, hidden), buf(TALL, mine), buf(8, LANES),
-            buf(2, groups, depth, block), buf(SLOTS, 2, piece, block), buf(held, SLOTS, 2, piece, block),
-            buf(landed, SLOTS, 2 * piece, block),
+            buf(2, groups, depth, block), buf(slots, 2, piece, block), buf(held, slots, 2, piece, block),
+            buf(landed, slots, 2 * piece, block),
             buf(groups, head_depth, block), buf(2, head_depth, block), buf(2, head_depth, block),
             buf(2 * head_depth, block),
-            buf(8, width), buf(groups, 8, width), buf(rows, 8, width),
-            buf(8, width), buf(groups, 8, width), buf(rows, 8, width),
-            buf(groups, long, width), buf(rows, long, width),
+            buf(16, LANES), buf(groups, 16, LANES), buf(rows, 16, LANES),
+            buf(2 * groups, LANES), buf(groups, 2 * groups, LANES), buf(rows, 2 * groups, LANES),
+            buf(groups, 4 * sections + 8, block), buf(groups, 4 * sections + 8, block), buf(4 * sections + 8, block),
+            buf(rows, 4 * sections + 8, block), buf(16, block), buf(groups, 16, block),
             dma((9,)), dma((9,)), dma((3,)),
         ] + [dma((units,))] * 16 + [
             dma((3, groups)), dma((3,)), dma((3,)), dma((3,)), dma((3,)), dma((1,)),
-            dma((3, 3)), dma((3, 3)), dma((3, rows - 1)), dma((3, rows - 1)),
-            dma((2, SLOTS)), dma((2, SLOTS)), dma((levels + 2, landed, SLOTS)), dma((levels + 2, landed, SLOTS)),
-            dma((levels, 3 * SLOTS)), dma((levels, 3 * SLOTS)), dma((3 * SLOTS,)),
+            dma((4, 3)), dma((4, 3)), dma((3, rows - 1)), dma((3, rows - 1)),
+            dma((2, slots)), dma((2, slots)), dma((levels + 2, landed, slots)), dma((levels + 2, landed, slots)),
+            dma((levels, 3 * slots)), dma((levels, 3 * slots)), dma((3 * slots,)),
             dma((2 * levels + 4,)), dma((2 * levels + 4,)), dma((1,)),
         ],
         compiler_params=pltpu.CompilerParams(
@@ -735,14 +792,14 @@
             row, row, sds((block, hidden), F32), sds((1, hidden), F32), sds((classes, hidden), F32),
             sds((1, classes), F32),
         ],
-        in_specs=[any_] * 4 + [vmem] * 4,
+        in_specs=[any_] * 4 + [vmem] * 5,
         out_specs=[vmem, any_, vmem, any_, any_, any_] + [vmem] * 9,
         scratch_shapes=[
             buf(3, sections, depth, block), buf(*features.shape), buf(8, LANES),
             dma((units + 1,)), dma((units + 1,)),
         ],
         compiler_params=pltpu.CompilerParams(vmem_limit_bytes=62 * 2**20),
-    )(*made[:8])
+    )(*made[:9])
 
 
 def local(

time: 383 us -> 350 us (0.914)
  Pallas kernels: 381 us -> 349 us
    pallas_call x1, Pallas kernels: 371 us -> 339 us  [layer(): pl.pallas_call(functools.partial(kernel, sections, rows, levels, classes)...]
where the time goes in v2:
time: 350 us
  Pallas kernels  349 us (100%)
    pallas_call x1, Pallas kernels, layer(): pl.pallas_call(functools.partial(kernel, sections, rows, levels, classes)...  339 us
    pallas_call x1, Pallas kernels, layer(): pl.pallas_call(functools.partial(finish_kernel, sections, classes), out_s...  9.54 us

profile of v2, /device:TPU:0, one launch (start us, length us, event | category | flops | bytes accessed | tf_op | source)
XLA Modules:
  0.0 350.1 jit_solution(14758596880664857183)
XLA Ops:
  1.3 339.1 %shard_map.280 = (f32[6,1024,128]{2,1,0:T(8,128)}, f32[6,1024,128]{2,1,0:T(8,128)}, f32[6,1024,128]{2,1,0:T(8,128)}, f32[1024,128]{1,0:T(8,128)}, f32[256,128]{1...) custom-call(f32[1024,128]{1,0:T(8,128)} %feat_ref.1, ...), custom_call_target="tpu_custom_call" | custom-call | tf_op jit(solution)/shard_map/pallas_call | solution.py:742
  340.4 9.5 %shard_map.281 = (f32[10,1024]{1,0:T(8,128)}, f32[1024,128]{1,0:T(8,128)}, f32[6,128]{1,0:T(8,128)}, f32[6,1024,128]{2,1,0:T(8,128)}, f32[6,1024,128]{2,1,0:T(8,...) custom-call(f32[6,1024,128]{2,1,0:T(8,128)} %get-tuple-element.39.gz, ...), custom_call_target="tpu_custom_call" | custom-call | tf_op jit(solution)/shard_map/pallas_call | solution.py:788

commit v3 on v2

--- a/solution.py
+++ b/solution.py
@@ -12,22 +12,28 @@
 LANES = 128
 PAR = 32
 TALL = 16
+RELAY, CORE, LOAD, GATE = 2, 4, 5, 6
 
 
 def cuts_of(levels):
     return 4 if levels < 6 else 2
 
 
-def early(levels):
-    return ((0, 3, 4, 7, 10), (2, 8), (3, 8)) if levels < 6 else ((5,),) * 3
+def orders(levels):
+    if levels == 3:
+        return "EAXAEAXEEAXX", "EXBABXAAAAAA", "BAAABABBXBXB"
+    return ("A" * (3 * cuts_of(levels) - 1) + "E",) * 3
+
+
+def order_of(kind, levels):
+    start = {"A": ["y", 0, 1], "E": [1, "y", 0], "B": ["y", 1, 0], "X": [0, "y", 1]}[kind]
+    return start + list(range(2, levels))
 
 
 def schedule(levels):
     if levels == 3:
-        return [1, 4, 7, 9, 11, 13, 15, 18]
-    sums = [1, 4, 7, 9] + [9 + k for k in range(1, levels - 1)]
-    gap = 2 if levels < 4 else 1
-    return sums + [sums[-1] + 1 + gap * k for k in range(levels)]
+        return [2, 6, 10, 13, 15, 17, 20, 27]
+    return list(range(1, 2 * levels + 3))
 
 
 def rings(levels):
@@ -264,7 +270,7 @@
         u = m - back_by
         return step + u // 3, u % 3
 
-    @pl.loop(0, sections + 2)
+    @pl.loop(0, sections + -(-GATE // 3))
     def _(step):
         for m in range(3):
 
@@ -274,7 +280,7 @@
                 x_copy(step, m).start()
                 z_copy(step, m).start()
 
-            s1, m1 = at(step, m, 1)
+            s1, m1 = at(step, m, RELAY)
 
             @pl.when((s1 >= 0) & (s1 < sections))
             def _():
@@ -283,7 +289,7 @@
                 b_copy(s1, m1).start()
                 c_copy(s1, m1).start()
 
-            s2, m2 = at(step, m, 2)
+            s2, m2 = at(step, m, CORE)
 
             @pl.when((s2 >= 0) & (s2 < sections))
             def _():
@@ -292,7 +298,7 @@
                 c_copy(s2, m2).wait_recv()
                 far_copy(s2, m2).start()
 
-            s3, m3 = at(step, m, 3)
+            s3, m3 = at(step, m, LOAD)
 
             @pl.when((s3 >= 0) & (s3 < sections))
             def _():
@@ -300,9 +306,9 @@
                 far_copy(s3, m3).wait_recv()
                 start(w_load(s3, m3))
 
-            if m == 0:
-                pl.when(step == 1)(arrange)
-            s4, m4 = at(step, m, 4)
+            if m == LOAD % 3:
+                pl.when(step == LOAD // 3)(arrange)
+            s4, m4 = at(step, m, GATE)
 
             @pl.when((s4 >= 0) & (s4 < sections))
             def _():
@@ -411,10 +417,10 @@
     peers = [(flip(r, 2**k), f) for k in range(levels)]
     piece = depth // cuts
     held, landed = rings(levels)
-    z_first = early(levels)
+    kinds = orders(levels)
 
     class Unit:
-        def __init__(self, step, j, by_z=False):
+        def __init__(self, step, j, kind="A"):
             m, cut = j // cuts, j % cuts
             span = pl.ds(cut * piece, piece)
             where = (step % 3) * slots + j
@@ -426,7 +432,7 @@
             self.rs_sems = [(rs_s.at[k, step % landed, j], rs_r.at[k, step % landed, j]) for k in range(levels + 2)]
             self.ag_sems = [(ag_s.at[k, where], ag_r.at[k, where]) for k in range(levels)]
             self.out_sem = out_l.at[where]
-            self.plan([1, "y", 0] + list(range(2, levels)) if by_z else ["y"] + list(range(levels)))
+            self.plan(order_of(kind, levels))
 
         def plan(self, order):
             self.moves, self.backs = [], []
@@ -485,7 +491,7 @@
             sems = [(hu_s.at[k], hu_r.at[k]) for k in range(2 * levels + 4)]
             self.core_sems, self.rs_sems, self.ag_sems = sems[:2], sems[2 : levels + 4], sems[levels + 4 :]
             self.out_sem = hu_l.at[0]
-            self.plan(["y"] + list(range(levels)))
+            self.plan(order_of("A", levels))
 
     def stage_core(unit):
         wait(unit.core_copies())
@@ -610,13 +616,12 @@
                         stage(HeadUnit())
 
                 groups = (s1 == 0, (s1 > 0) & (s1 < sections - 1), s1 == sections - 1)
-                for by_z in (False, True):
-                    active = [g for g, early_units in zip(groups, z_first, strict=True) if (j1 in early_units) == by_z]
-                    if active:
-
-                        @pl.when(functools.reduce(jnp.logical_or, active))
-                        def _():
-                            stage(Unit(s1, j1, by_z))
+                for kind in sorted({row[j1] for row in kinds}):
+                    active = [g for g, row in zip(groups, kinds, strict=True) if row[j1] == kind]
+
+                    @pl.when(functools.reduce(jnp.logical_or, active))
+                    def _():
+                        stage(Unit(s1, j1, kind))
 
             if j == 0:
 
@@ -684,19 +689,18 @@
     gz_ref, gr_ref, go_ref, gfeat_ref, ghead_ref, logit_ref, tiny_ref, own_ref, aux_ref,
     logit_out, gfeat_out, gmask_out, gz_out, gr_out, go_out, bz_out, br_out, bo_out,
     gain_out, shift_out, ghead_out, bhead_out, wout_out, bout_out,
-    big, feat, head, load, store,
+    store,
 ):
     f = lax.axis_index("feat")
-    pairs = [(feat, gfeat_ref, gfeat_out)] + [
-        (big.at[m, s], src.at[s], dst.at[s])
+    pairs = [(gfeat_ref, gfeat_out)] + [
+        (src.at[s], dst.at[s])
         for s in range(sections)
-        for m, (src, dst) in enumerate(((gz_ref, gz_out), (gr_ref, gr_out), (go_ref, go_out)))
+        for src, dst in ((gz_ref, gz_out), (gr_ref, gr_out), (go_ref, go_out))
     ]
-    loads = [pltpu.make_async_copy(src, held, load.at[k]) for k, (held, src, _) in enumerate(pairs)]
-    stores = [pltpu.make_async_copy(held, dst, store.at[k]) for k, (held, _, dst) in enumerate(pairs)]
-    for copy in loads:
+    stores = [pltpu.make_async_copy(src, dst, store.at[k]) for k, (src, dst) in enumerate(pairs)]
+    for copy in stores:
         copy.start()
-    block = feat.shape[1]
+    block = gfeat_ref.shape[1]
     hidden = bhead_out.shape[1]
     logit_out[...] = logit_ref[0:classes]
     for k, out in enumerate((bz_out, br_out, bo_out, gmask_out)):
@@ -708,9 +712,6 @@
     wout_out[...] = aux_ref[0:classes]
     bhead_out[...] = aux_ref[classes : classes + 1]
     bout_out[...] = aux_ref[classes + 1 : classes + 2, 0:classes]
-    for load_, store_ in zip(loads, stores, strict=True):
-        load_.wait()
-        store_.start()
     for copy in stores:
         copy.wait()
 
@@ -735,6 +736,7 @@
     dma = pltpu.SemaphoreType.DMA
     any_, vmem = pl.BlockSpec(memory_space=pl.ANY), pl.BlockSpec(memory_space=pltpu.VMEM)
     grad = sds((sections, depth, block), F32)
+    held_grad = pltpu.VMEM((sections, depth, block), F32)
 
     def buf(*shape):
         return pltpu.VMEM(shape, F32)
@@ -742,17 +744,17 @@
     made = pl.pallas_call(
         functools.partial(kernel, sections, rows, levels, classes),
         out_shape=[
-            grad, grad, grad,
-            sds(features.shape, F32),
-            sds((head_depth, block), F32),
-            sds((TALL, groups * mine), F32),
-            sds((2 * groups, block), F32),
-            sds((4 * sections, block), F32),
-            sds((TALL, hidden), F32),
+            held_grad, held_grad, held_grad,
+            pltpu.VMEM(features.shape, F32),
+            pltpu.VMEM((head_depth, block), F32),
+            pltpu.VMEM((TALL, groups * mine), F32),
+            pltpu.VMEM((2 * groups, block), F32),
+            pltpu.VMEM((4 * sections, block), F32),
+            pltpu.VMEM((TALL, hidden), F32),
             sds((sections, 3, groups, depth, block), F32),
         ],
         in_specs=[any_] * 5 + [pl.BlockSpec(memory_space=pltpu.SMEM)] + [vmem] * 11,
-        out_specs=[any_] * 5 + [vmem] * 4 + [any_],
+        out_specs=[vmem] * 9 + [any_],
         scratch_shapes=[
             buf(mine, width), buf(groups, PAR, block), buf(PAR, width), buf(sections + 1, mine, width),
             buf(sections, mine, width), buf(sections, mine, width), buf(sections, mine, width),
@@ -777,7 +779,7 @@
             dma((2 * levels + 4,)), dma((2 * levels + 4,)), dma((1,)),
         ],
         compiler_params=pltpu.CompilerParams(
-            collective_id=0, has_side_effects=True, vmem_limit_bytes=62 * 2**20
+            collective_id=0, has_side_effects=True, vmem_limit_bytes=52 * 2**20
         ),
     )(
         features, w_update, w_reset, w_candidate, w_head, counts, validity[None], mask_logits, b_update, b_reset,
@@ -792,13 +794,10 @@
             row, row, sds((block, hidden), F32), sds((1, hidden), F32), sds((classes, hidden), F32),
             sds((1, classes), F32),
         ],
-        in_specs=[any_] * 4 + [vmem] * 5,
+        in_specs=[vmem] * 3 + [vmem] + [vmem] * 5,
         out_specs=[vmem, any_, vmem, any_, any_, any_] + [vmem] * 9,
-        scratch_shapes=[
-            buf(3, sections, depth, block), buf(*features.shape), buf(8, LANES),
-            dma((units + 1,)), dma((units + 1,)),
-        ],
-        compiler_params=pltpu.CompilerParams(vmem_limit_bytes=62 * 2**20),
+        scratch_shapes=[dma((units + 1,))],
+        compiler_params=pltpu.CompilerParams(vmem_limit_bytes=16 * 2**20),
     )(*made[:9])
 
 

time: 350 us -> 341 us (0.974)
  Pallas kernels: 349 us -> 339 us
    pallas_call x1, Pallas kernels: 9.54 us -> 4.63 us  [layer(): pl.pallas_call(functools.partial(finish_kernel, sections, classes), out_s...]
    pallas_call x1, Pallas kernels: 339 us -> 335 us  [layer(): pl.pallas_call(functools.partial(kernel, sections, rows, levels, classes)...]
where the time goes in v3:
time: 341 us
  Pallas kernels  339 us (99%)
    pallas_call x1, Pallas kernels, layer(): pl.pallas_call(functools.partial(kernel, sections, rows, levels, classes)...  335 us

profile of v3, /device:TPU:0, one launch (start us, length us, event | category | flops | bytes accessed | tf_op | source)
XLA Modules:
  0.0 340.6 jit_solution(11168650561949501638)
XLA Ops:
  1.3 334.6 %shard_map.280 = (f32[6,1024,128]{2,1,0:T(8,128)S(1)}, f32[6,1024,128]{2,1,0:T(8,128)S(1)}, f32[6,1024,128]{2,1,0:T(8,128)S(1)}, f32[1024,128]{1,0:T(8,128)S(1)}...) custom-call(f32[1024,128]{1,0:T(8,128)} %feat_ref.1, ...), custom_call_target="tpu_custom_call" | custom-call | tf_op jit(solution)/shard_map/pallas_call | solution.py:744
  335.9 4.6 %shard_map.281 = (f32[10,1024]{1,0:T(8,128)}, f32[1024,128]{1,0:T(8,128)}, f32[6,128]{1,0:T(8,128)}, f32[6,1024,128]{2,1,0:T(8,128)}, f32[6,1024,128]{2,1,0:T(8,...) custom-call(f32[6,1024,128]{2,1,0:T(8,128)S(1)} %get-tuple-element.3, ...), custom_call_target="tpu_custom_call" | custom-call | tf_op jit(solution)/shard_map/pallas_call | solution.py:790

commit v4 on v3

--- a/solution.py
+++ b/solution.py
@@ -12,7 +12,7 @@
 LANES = 128
 PAR = 32
 TALL = 16
-RELAY, CORE, LOAD, GATE = 2, 4, 5, 6
+RELAY, CORE, LOAD, GATE = 1, 3, 4, 5
 
 
 def cuts_of(levels):
@@ -32,7 +32,7 @@
 
 def schedule(levels):
     if levels == 3:
-        return [2, 6, 10, 13, 15, 17, 20, 27]
+        return [3, 7, 11, 14, 16, 18, 21, 28]
     return list(range(1, 2 * levels + 3))
 
 
@@ -131,7 +131,8 @@
     others = (core, far, both)
     rx, rz = flip(r, 1), flip(r, 2)
     quarter = depth // 4
-    cut_b, cut_c = 3 * quarter // 8, 3 * quarter // 8 + 5 * quarter // 16
+    cut_b, cut_c = quarter // 8, quarter // 8 + 7 * quarter // 16
+    final = sections - 1
     q = 2 * (r % 2) + (r // 2) % 2
     q_x, q_z, q_d = flip(q, 2), flip(q, 1), flip(flip(q, 1), 2)
 
@@ -170,8 +171,8 @@
         u, span = 3 * s + m, rows_of(q, 0, quarter)
         return remote(weights[m].at[s, span], wfull.at[s, m, f, span], fy_s.at[u], fy_r.at[u], (r, far))
 
-    def a_copy(s, m):
-        u, span = 3 * s + m, rows_of(q_d, 0, cut_b)
+    def a_copy(s, m, whole=False):
+        u, span = 3 * s + m, rows_of(q_d, 0, quarter if whole else cut_b)
         return remote(weights[m].at[s, span], wfull.at[s, m, f, span], a_s.at[u], a_r.at[u], (r, far))
 
     def own_copy(s, m):
@@ -214,19 +215,20 @@
         for copy in copies:
             copy.wait()
 
-    def send_own(s):
+    def send_own(s, whole=False):
         for m in range(3):
             y_copy(s, m).start()
-            a_copy(s, m).start()
+            a_copy(s, m, whole).start()
             own_copy(s, m).start()
 
     send_own(0)
     start(firsts + locals_)
 
-    @pl.loop(1, sections)
+    @pl.loop(1, final)
     def _(s):
         send_own(s)
 
+    send_own(final, True)
     start(heads)
 
     def arrange():
@@ -286,18 +288,26 @@
             def _():
                 x_copy(s1, m1).wait_recv()
                 z_copy(s1, m1).wait_recv()
+
+            @pl.when((s1 >= 0) & (s1 < final))
+            def _():
                 b_copy(s1, m1).start()
                 c_copy(s1, m1).start()
 
             s2, m2 = at(step, m, CORE)
 
-            @pl.when((s2 >= 0) & (s2 < sections))
+            @pl.when((s2 >= 0) & (s2 < final))
             def _():
                 a_copy(s2, m2).wait_recv()
                 b_copy(s2, m2).wait_recv()
                 c_copy(s2, m2).wait_recv()
                 far_copy(s2, m2).start()
 
+            @pl.when(s2 == final)
+            def _():
+                a_copy(s2, m2, True).wait_recv()
+                far_copy(s2, m2).start()
+
             s3, m3 = at(step, m, LOAD)
 
             @pl.when((s3 >= 0) & (s3 < sections))
@@ -326,18 +336,26 @@
             for k in range(1, rows)
         ]
 
-    def sum_all(n, value, src, feat_slots, row_slots, merge):
+    unsent = []
+
+    def sum_all(n, value, src, feat_slots, row_slots, merge, meanwhile):
         feat_slots[f] = value
-        src[...] = value
-        copies = feat_step(n, src, feat_slots)
+        src[0] = value
+        copies = feat_step(n, src.at[0], feat_slots)
         start(copies)
-        wait(copies)
+        unsent.extend(copies)
+        for copy in copies:
+            copy.wait_recv()
         value = merge(feat_slots)
         row_slots[r] = value
-        src[...] = value
-        copies = rows_step(n, src, row_slots)
+        src[1] = value
+        copies = rows_step(n, src.at[1], row_slots)
         start(copies)
-        return copies
+        unsent.extend(copies)
+        done = meanwhile()
+        for copy in copies:
+            copy.wait_recv()
+        return merge(row_slots), done
 
     for m in (2, 0, 1):
         start(w_load(sections - 1, m))
@@ -345,44 +363,40 @@
     place = lax.broadcasted_iota(jnp.int32, (1, mine), 1) + f * mine
     flat = jnp.where(place < count_ref[0], 1.0, 0.0) * valid_ref[:, here].astype(F32)
     column = jnp.transpose(jnp.broadcast_to(flat, (8, mine)))[:, 0:1]
-    wout_buf[...] = jnp.zeros_like(wout_buf)
-    wout_buf[0:classes] = wout_ref[...]
-    dlog_buf[...] = jnp.zeros_like(dlog_buf)
-    dlog_buf[0:classes] = cot_ref[:, here] * flat
-    turn[...] = jnp.zeros_like(turn)
-    turn[0:1, 0:classes] = bout_ref[...]
-    b_out = jnp.transpose(turn[...])[0:TALL, 0:1]
     current = hs[sections]
     count = jnp.sum(column, axis=0, keepdims=True)
     sums = jnp.sum(column * current, axis=0, keepdims=True)
     gap = current - sums / jnp.maximum(count, 1.0)
     square = jnp.sum(column * gap * gap, axis=0, keepdims=True)
-    rest = jnp.zeros((ex_a.shape[0] - 2 * blocks - 1, LANES), F32)
+    rest = jnp.zeros((ex_a.shape[1] - 2 * blocks - 1, LANES), F32)
     stats = jnp.concatenate(stack(sums) + stack(square) + [jnp.broadcast_to(count, (1, LANES)), rest], axis=0)
-    merge = functools.partial(merge_stats, blocks)
-    wait(sum_all(0, stats, ex_a, ex_a_feat, ex_a_rows, merge))
-    stats = merge(ex_a_rows)
+
+    def prepare():
+        wout_buf[...] = jnp.zeros_like(wout_buf)
+        wout_buf[0:classes] = wout_ref[...]
+        dlog_buf[...] = jnp.zeros_like(dlog_buf)
+        dlog_buf[0:classes] = cot_ref[:, here] * flat
+        turn[...] = jnp.zeros_like(turn)
+        turn[0:1, 0:classes] = bout_ref[...]
+        b_out = jnp.transpose(turn[...])[0:TALL, 0:1]
+        for copy in heads:
+            copy.wait_recv()
+        d_log = split(dlog_buf[...])
+        w_out = split(wout_buf[...])
+        return d_log, w_out, dot3(d_log, w_out, TN), b_out
+
+    stats, prepared = sum_all(0, stats, ex_a, ex_a_feat, ex_a_rows, functools.partial(merge_stats, blocks), prepare)
+    d_log, w_out, d_hidden, b_out = prepared
     count = stats[2 * blocks : 2 * blocks + 1, 0:1]
     inv_std = lax.rsqrt(unstack(stats[blocks : 2 * blocks]) / count + 1e-05)
     x_hat[...] = (current - unstack(stats[0:blocks]) / count) * inv_std
     gain, shift = par[4 * sections : 4 * sections + 1], par[4 * sections + 1 : 4 * sections + 2]
     normed = split(x_hat[...] * gain + shift)
-    for copy in heads:
-        copy.wait_recv()
     w_head = split(whead[...])
     act = dot3(normed, w_head, NN) + bhead_ref[...]
     phi = 0.5 * (1.0 + lax.erf(act * 0.7071067811865476))
-    hidden = split(act * phi)
     slope = phi + act * (jnp.exp(-0.5 * act * act) * 0.3989422804014327)
-    w_out = split(wout_buf[...])
-    logit_buf[f] = (dot3(w_out, hidden, NT) + b_out) * flat
-    logit_copies = [
-        remote(logit_buf.at[f], logit_buf.at[f], logit_s.at[k], logit_r.at[k], (r, peer))
-        for k, peer in enumerate(others)
-    ]
-    start(logit_copies)
-    d_log = dlog_buf[...]
-    d_act = dot3(split(d_log), w_out, TN) * slope
+    d_act = d_hidden * slope
     d_act2 = split(d_act)
     d_normed = dot3(d_act2, w_head, NT)
     sums = jnp.concatenate(
@@ -391,26 +405,29 @@
         axis=0,
     )
     dh[...] = d_normed
-    copies = sum_all(1, sums, ex_b, ex_b_feat, ex_b_rows, sum_slots)
-    vec[...] = jnp.zeros_like(vec)
     hid = act.shape[1]
     aux = 4 * sections
-    vec[aux : aux + TALL, 0:hid] = dot3(split(d_log), hidden, NN)
-    vec[aux + classes : aux + classes + 1, 0:hid] = jnp.sum(d_act, axis=0, keepdims=True)
-    ones = jnp.ones((8, mine), F32)
-    vec[aux + classes + 1 : aux + classes + 2, 0:TALL] = dot3(split(ones), split(d_log), NT)[0:1]
-    grad = dot3(normed, d_act2, TN)
-    for b in range(blocks):
-        for t in range(hid // LANES):
-            h_grads[b, t * LANES : (t + 1) * LANES] = grad[
-                b * LANES : (b + 1) * LANES, t * LANES : (t + 1) * LANES
-            ]
-    wait(copies)
-    sums = sum_slots(ex_b_rows)
-    g_gain, g_shift = unstack(sums[0:blocks]), unstack(sums[blocks:])
-    dh[...] = inv_std * (dh[...] * gain - column / count * gain * (g_shift + x_hat[...] * g_gain))
-    tiny_out[...] = sums
-    gin[...] = jnp.zeros_like(gin)
+    logit_copies = [
+        remote(logit_buf.at[f], logit_buf.at[f], logit_s.at[k], logit_r.at[k], (r, peer))
+        for k, peer in enumerate(others)
+    ]
+
+    def head_rest():
+        hidden = split(act * phi)
+        logit_buf[f] = (dot3(w_out, hidden, NT) + b_out) * flat
+        start(logit_copies)
+        vec[...] = jnp.zeros_like(vec)
+        vec[aux : aux + TALL, 0:hid] = dot3(d_log, hidden, NN)
+        vec[aux + classes : aux + classes + 1, 0:hid] = jnp.sum(d_act, axis=0, keepdims=True)
+        ones = split(jnp.ones((8, mine), F32))
+        vec[aux + classes + 1 : aux + classes + 2, 0:TALL] = dot3(ones, d_log, NT)[0:1]
+        grad = dot3(normed, d_act2, TN)
+        for b in range(blocks):
+            for t in range(hid // LANES):
+                h_grads[b, t * LANES : (t + 1) * LANES] = grad[
+                    b * LANES : (b + 1) * LANES, t * LANES : (t + 1) * LANES
+                ]
+        start(HeadUnit().core_copies())
 
     outs = (go_out, gz_out, gr_out)
     which = (2, 0, 1)
@@ -529,7 +546,7 @@
     def back(m, left, t):
         return dot3(left, split(weight[which[m], t * half : (t + 1) * half, :]), NT)
 
-    def compute(step, m):
+    def compute(step, m, ready):
         s = sections - 1 - step
         u = 3 * step + m
         wait(w_load(s, which[m]))
@@ -541,6 +558,7 @@
             d_out = dh[...] * z * (1.0 - c * c)
             vec[pl.ds(2 * sections + s, 1), :] = jnp.sum(d_out, axis=0, keepdims=True)
             outer(m, u, d_out)
+            ready()
             left = split(d_out)
             for t in range(4):
                 d_in[:, t * half : (t + 1) * half] = back(m, left, t)
@@ -551,6 +569,7 @@
             d_up = dh[...] * (c - h) * z * (1.0 - z)
             vec[pl.ds(s, 1), :] = jnp.sum(d_up, axis=0, keepdims=True)
             outer(m, u, d_up)
+            ready()
             dh[...] = dh[...] * (1.0 - z) + d_in[:, 0:width] * reset
             left = split(d_up)
             for t in range(4):
@@ -563,6 +582,7 @@
             d_r = d_reset[...]
             vec[pl.ds(sections + s, 1), :] = jnp.sum(d_r, axis=0, keepdims=True)
             outer(m, u, d_r)
+            ready()
             left = split(d_r)
             for t in range(4):
                 cols = slice(t % 2 * half, (t % 2 + 1) * half)
@@ -589,7 +609,11 @@
     vec_last = feat_step(3, ex_d, ex_d_feat)
     spread = hid // LANES
 
-    start(HeadUnit().core_copies())
+    sums, _ = sum_all(1, sums, ex_b, ex_b_feat, ex_b_rows, sum_slots, head_rest)
+    g_gain, g_shift = unstack(sums[0:blocks]), unstack(sums[blocks:])
+    dh[...] = inv_std * (dh[...] * gain - column / count * gain * (g_shift + x_hat[...] * g_gain))
+    tiny_out[...] = sums
+    gin[...] = jnp.zeros_like(gin)
 
     def before(step, j, back_by):
         u = j - back_by
@@ -603,9 +627,13 @@
 
             @pl.when(step < sections)
             def _():
+                def ready():
+                    start(Unit(step, j).core_copies())
+
                 if j % cuts == 0:
-                    compute(step, j // cuts)
-                start(Unit(step, j).core_copies())
+                    compute(step, j // cuts, ready)
+                else:
+                    ready()
 
             for delay, stage in zip(delays, stages, strict=True):
                 s1, j1 = before(step, j, delay)
@@ -677,10 +705,19 @@
     @pl.loop(0, sections)
     def _(s):
         for m in range(3):
-            for copy in (y_copy, a_copy, own_copy, x_copy, z_copy, b_copy, c_copy, far_copy):
+            for copy in (y_copy, own_copy, x_copy, z_copy, far_copy):
                 copy(s, m).wait_send()
 
-    for copy in firsts + heads:
+    @pl.loop(0, final)
+    def _(s):
+        for m in range(3):
+            for copy in (a_copy, b_copy, c_copy):
+                copy(s, m).wait_send()
+
+    for m in range(3):
+        a_copy(final, m, True).wait_send()
+
+    for copy in firsts + heads + unsent:
         copy.wait_send()
 
 
@@ -766,8 +803,8 @@
             buf(landed, slots, 2 * piece, block),
             buf(groups, head_depth, block), buf(2, head_depth, block), buf(2, head_depth, block),
             buf(2 * head_depth, block),
-            buf(16, LANES), buf(groups, 16, LANES), buf(rows, 16, LANES),
-            buf(2 * groups, LANES), buf(groups, 2 * groups, LANES), buf(rows, 2 * groups, LANES),
+            buf(2, 16, LANES), buf(groups, 16, LANES), buf(rows, 16, LANES),
+            buf(2, 2 * groups, LANES), buf(groups, 2 * groups, LANES), buf(rows, 2 * groups, LANES),
             buf(groups, 4 * sections + 8, block), buf(groups, 4 * sections + 8, block), buf(4 * sections + 8, block),
             buf(rows, 4 * sections + 8, block), buf(16, block), buf(groups, 16, block),
             dma((9,)), dma((9,)), dma((3,)),

time: 341 us -> 338 us (level)
  no operation moved by 1% of the time
where the time goes in v4:
time: 338 us
  Pallas kernels  336 us (99%)
    pallas_call x1, Pallas kernels, layer(): pl.pallas_call(functools.partial(kernel, sections, rows, levels, classes)...  331 us

profile of v4, /device:TPU:0, one launch (start us, length us, event | category | flops | bytes accessed | tf_op | source)
XLA Modules:
  0.0 337.6 jit_solution(2574859784701653121)
XLA Ops:
  1.3 331.5 %shard_map.280 = (f32[6,1024,128]{2,1,0:T(8,128)S(1)}, f32[6,1024,128]{2,1,0:T(8,128)S(1)}, f32[6,1024,128]{2,1,0:T(8,128)S(1)}, f32[1024,128]{1,0:T(8,128)S(1)}...) custom-call(f32[1024,128]{1,0:T(8,128)} %feat_ref.1, ...), custom_call_target="tpu_custom_call" | custom-call | tf_op jit(solution)/shard_map/pallas_call | solution.py:781
  332.8 4.6 %shard_map.281 = (f32[10,1024]{1,0:T(8,128)}, f32[1024,128]{1,0:T(8,128)}, f32[6,128]{1,0:T(8,128)}, f32[6,1024,128]{2,1,0:T(8,128)}, f32[6,1024,128]{2,1,0:T(8,...) custom-call(f32[6,1024,128]{2,1,0:T(8,128)S(1)} %get-tuple-element.3, ...), custom_call_target="tpu_custom_call" | custom-call | tf_op jit(solution)/shard_map/pallas_call | solution.py:827

commit v5 on v4

--- a/solution.py
+++ b/solution.py
@@ -12,7 +12,7 @@
 LANES = 128
 PAR = 32
 TALL = 16
-RELAY, CORE, LOAD, GATE = 1, 3, 4, 5
+RELAY, CORE, LOAD, GATE = 1, 2, 3, 4
 
 
 def cuts_of(levels):

time: 338 us -> 336 us (level)
  no operation moved by 1% of the time
where the time goes in v5:
time: 336 us
  Pallas kernels  335 us (100%)
    pallas_call x1, Pallas kernels, layer(): pl.pallas_call(functools.partial(kernel, sections, rows, levels, classes)...  330 us

profile of v5, /device:TPU:0, one launch (start us, length us, event | category | flops | bytes accessed | tf_op | source)
XLA Modules:
  0.0 336.1 jit_solution(17376485100758215239)
XLA Ops:
  1.3 330.0 %shard_map.280 = (f32[6,1024,128]{2,1,0:T(8,128)S(1)}, f32[6,1024,128]{2,1,0:T(8,128)S(1)}, f32[6,1024,128]{2,1,0:T(8,128)S(1)}, f32[1024,128]{1,0:T(8,128)S(1)}...) custom-call(f32[1024,128]{1,0:T(8,128)} %feat_ref.1, ...), custom_call_target="tpu_custom_call" | custom-call | tf_op jit(solution)/shard_map/pallas_call | solution.py:781
  331.3 4.6 %shard_map.281 = (f32[10,1024]{1,0:T(8,128)}, f32[1024,128]{1,0:T(8,128)}, f32[6,128]{1,0:T(8,128)}, f32[6,1024,128]{2,1,0:T(8,128)}, f32[6,1024,128]{2,1,0:T(8,...) custom-call(f32[6,1024,128]{2,1,0:T(8,128)S(1)} %get-tuple-element.3, ...), custom_call_target="tpu_custom_call" | custom-call | tf_op jit(solution)/shard_map/pallas_call | solution.py:827
